TPU v7x, 32 devices: a whole 2x2x4 slice. The times are simulated.
32 devices in a mesh: parts: 2 (over y), blk: 4 (over z), rhs: 2 (over x), sub: 2 (over core).
Axes of the slice: x: 2, y: 2, z: 4, core: 2. Of those that a mesh axis runs over, the one named last changes fastest.
Arguments:
- currents: bfloat16 [2, 80, 24576], P(None, None, ('parts', 'blk', 'rhs')), parts along dimension 2, may hold values from -6 to 6
- tri_cent: float32 [3, 16384], P(None, 'parts'), parts along dimension 1, may hold values from 0 to 10
- edge_tris: int32 [2, 24576], P(None, 'parts'), parts along dimension 1, may hold values from 0 to 8191
- edge_len: float32 [24576], P('parts'), parts along dimension 0, may hold values from 0.5 to 2
- near_col: int32 [384, 4], P(('parts', 'blk', 'sub'), 'rhs'), parts along dimension 0, may hold values from 0 to 191, as said below
- near_val: bfloat16 [384, 4, 64, 128], P(('parts', 'blk', 'sub'), 'rhs'), parts along dimension 0, may hold values from -0.25 to 0.25
- refine_map: int32 [24576], P('parts'), parts along dimension 0, may hold values from 0 to 12287, as said below
- dual_blocks: bfloat16 [384, 64, 128], P(('parts', 'blk', 'sub')), parts along dimension 0, may hold values from -0.5 to 0.5
Outputs:
- calderon: float32 [2, 80, 24576], P(None, 'rhs', ('parts', 'blk', 'sub')), parts along dimension 2
There are 2 independent parts, one for each index of `parts`. A program takes and returns all parts, laid end to end along the dimension named above; each array names one. Nothing has to cross between parts.
Inputs may be any that keep to these rules, and one draw needn't show every extreme that they name: near_col[b, j] lies in (g * 2 + j // 2) * 24 to (g * 2 + j // 2 + 1) * 24 - 1, where g = b // 48. `refine_map`: a permutation; for all s, o below 8, exactly 192 of the entries s * 1536 to (s + 1) * 1536 - 1 lie in o * 1536 to (o + 1) * 1536 - 1.
All inputs are finite; a program needn't handle non-finite values.
Results may differ from a plain program's by a relative error of at most 0.004.
Values may be sent and summed in bfloat16 or wider, within the bound.
A program may use at most 64 MiB of HBM per device.

v0:
```python
import math

import jax
import jax.numpy as jnp
from jax import lax
from jax.sharding import PartitionSpec as P

ROWS_DEV = 1536
BS = 64


WAVE_NUMBER = 2.0 * math.pi
SOFTENING = 0.1
SPAN_SCALE = 3.0
CHARGE_TERM = 0.5


def geometry_span(first_id, width, tri_cent, edge_tris, edge_len):
    plus_ids = lax.dynamic_slice_in_dim(edge_tris[0], first_id, width, 0)
    minus_ids = lax.dynamic_slice_in_dim(edge_tris[1], first_id, width, 0)
    plus_tri = jnp.take(tri_cent, plus_ids, axis=1)
    minus_tri = jnp.take(tri_cent, minus_ids, axis=1)
    lengths = lax.dynamic_slice_in_dim(edge_len, first_id, width, 0)
    return (0.5 * (plus_tri + minus_tri), minus_tri - plus_tri, lengths)


def kernel_tile(columns, rowset, count_all):
    col_pos, col_dir, col_len = columns
    row_pos, row_dir, row_len = rowset
    squared = jnp.zeros((col_pos.shape[1], row_pos.shape[1]), jnp.float32)
    aligned = jnp.zeros((col_pos.shape[1], row_pos.shape[1]), jnp.float32)
    for component in range(3):
        offset = col_pos[component][:, None] - row_pos[component][None, :]
        squared = squared + offset * offset
        aligned = aligned + col_dir[component][:, None] * row_dir[component][None, :]
    distance = jnp.sqrt(squared + SOFTENING * SOFTENING)
    weight = (
        col_len[:, None]
        * row_len[None, :]
        * (aligned / (SPAN_SCALE * SPAN_SCALE) - CHARGE_TERM)
        / (distance * math.sqrt(count_all))
    )
    phases = WAVE_NUMBER * distance
    return jnp.concatenate(
        [
            (weight * jnp.cos(phases)).astype(jnp.bfloat16),
            (weight * jnp.sin(phases)).astype(jnp.bfloat16),
        ],
        0,
    )


def complex_pairs(real_part, imag_part, where_at):
    return jnp.stack(
        [jnp.stack([real_part, -imag_part], where_at), jnp.stack([imag_part, real_part], where_at)],
        where_at,
    )


def panel_product(totals, cur_panel, first_id, rowset, tables, count_all):
    columns = geometry_span(first_id, cur_panel.shape[2], tables[0], tables[1], tables[2])
    tile_pair = kernel_tile(columns, rowset, count_all)
    stacked = jnp.concatenate(
        [
            jnp.concatenate([cur_panel[0], -cur_panel[1]], 1),
            jnp.concatenate([cur_panel[1], cur_panel[0]], 1),
        ],
        0,
    )
    return totals + jnp.dot(stacked, tile_pair, preferred_element_type=jnp.float32)


def fold_panels(shard_width, group_cols, col_base, rowset, tables, count_all):

    def folder(totals, arrived, begin_at):
        shard_count = arrived.shape[2] // shard_width
        shards = jnp.moveaxis(
            arrived.reshape(arrived.shape[0], arrived.shape[1], shard_count, shard_width), 2, 0
        )
        first_shard = begin_at // shard_width

        def advance(running, scanned):
            cur_panel, offset = scanned
            first_id = offset * group_cols + col_base
            return (panel_product(running, cur_panel, first_id, rowset, tables, count_all), None)

        result, unused = lax.scan(
            advance, totals, (shards, jnp.arange(shard_count, dtype=jnp.int32))
        )
        return result

    return folder


def near_terms(currents, near_col, near_val):
    angle_count = currents.shape[1]
    block_count = currents.shape[2] // BS
    row_blocks = near_col.shape[0]
    per_tile = near_col.shape[1]
    blocks = currents.reshape(2 * angle_count, block_count, BS)
    local_block = near_col % block_count
    onehot = (
        local_block[:, :, None] == jnp.arange(block_count, dtype=jnp.int32)[None, None, :]
    ).astype(jnp.bfloat16)
    chosen = jnp.einsum("rjk,ckn->rjcn", onehot, blocks, preferred_element_type=jnp.float32).astype(
        jnp.bfloat16
    )
    chosen = chosen.reshape(row_blocks, per_tile, 2, angle_count, BS)
    paired = complex_pairs(chosen[:, :, 0], chosen[:, :, 1], 0)
    values = near_val.reshape(row_blocks, per_tile, BS, 2, BS)
    near_sum = jnp.einsum("rjmtn,otrjan->oarm", values, paired, preferred_element_type=jnp.float32)
    return near_sum.reshape(2, angle_count, row_blocks * BS)


def dual_apply(moved, dual_blocks):
    angle_count = moved.shape[1]
    row_blocks = dual_blocks.shape[0]
    blocked = moved.reshape(2, angle_count, row_blocks, BS)
    paired = complex_pairs(blocked[0], blocked[1], 0)
    operator = dual_blocks.reshape(row_blocks, BS, 2, BS)
    result = jnp.einsum("bmtn,otabn->oabm", operator, paired, preferred_element_type=jnp.float32)
    return result.reshape(2, angle_count, row_blocks * BS)


def body(currents, tri_cent, edge_tris, edge_len, near_col, near_val, refine_map, dual_blocks):
    blk_count = lax.axis_size("blk")
    rhs_count = lax.axis_size("rhs")
    sub_count = lax.axis_size("sub")
    blk_index = lax.axis_index("blk")
    rhs_index = lax.axis_index("rhs")
    sub_index = lax.axis_index("sub")
    angle_count = currents.shape[1]
    tile_cols = currents.shape[2]
    group_cols = tile_cols * rhs_count
    count_all = group_cols * blk_count
    tables = (tri_cent, edge_tris, edge_len)
    near_sum = near_terms(currents, near_col, near_val)
    first_row = (blk_index * sub_count + sub_index) * ROWS_DEV
    rowset = geometry_span(first_row, ROWS_DEV, tri_cent, edge_tris, edge_len)
    empty = jnp.zeros((2 * angle_count, ROWS_DEV), jnp.float32)
    folder = fold_panels(tile_cols, group_cols, rhs_index * tile_cols, rowset, tables, count_all)
    far_sum = folder(empty, lax.all_gather(currents, "blk", axis=2, tiled=True), jnp.int32(0))
    local_sum = far_sum.reshape(2, angle_count, ROWS_DEV) + near_sum
    product = lax.psum_scatter(local_sum, "rhs", scatter_dimension=1, tiled=True)
    coarse_product = product.astype(jnp.bfloat16)
    part_angles = coarse_product.shape[1]
    channels = 2 * part_angles
    flat_rows = coarse_product.reshape(channels, ROWS_DEV)
    owners = blk_count * sub_count
    slot_rows = ROWS_DEV // owners
    my_owner = blk_index * sub_count + sub_index
    row_range = jnp.arange(ROWS_DEV, dtype=jnp.int32)
    owner_range = jnp.arange(owners, dtype=jnp.int32)
    earlier = (row_range[:, None] > row_range[None, :]).astype(jnp.bfloat16)
    own_map = lax.dynamic_slice_in_dim(refine_map, my_owner * ROWS_DEV, ROWS_DEV, 0)
    target_owner = own_map // ROWS_DEV
    owner_onehot = (target_owner[:, None] == owner_range[None, :]).astype(jnp.bfloat16)
    prior_counts = jnp.dot(earlier, owner_onehot, preferred_element_type=jnp.float32)
    send_rank = jnp.sum(prior_counts * owner_onehot.astype(jnp.float32), axis=1).astype(jnp.int32)
    send_slot = target_owner * slot_rows + send_rank
    send_perm = (send_slot[:, None] == row_range[None, :]).astype(jnp.bfloat16)
    outgoing = jnp.dot(flat_rows, send_perm, preferred_element_type=jnp.float32).astype(
        jnp.bfloat16
    )
    arrived = lax.all_to_all(
        outgoing.reshape(channels, owners, slot_rows),
        ("blk", "sub"),
        split_axis=1,
        concat_axis=1,
        tiled=True,
    )
    source_table = refine_map.reshape(owners, ROWS_DEV)
    bound_here = source_table // ROWS_DEV == my_owner
    recv_counts = jnp.dot(
        bound_here.astype(jnp.bfloat16), jnp.transpose(earlier), preferred_element_type=jnp.float32
    )
    recv_rank = recv_counts.astype(jnp.int32)
    landing = source_table % ROWS_DEV
    slot_range = jnp.arange(slot_rows, dtype=jnp.int32)
    matches = bound_here[:, :, None] & (recv_rank[:, :, None] == slot_range[None, None, :])
    slot_position = jnp.sum(jnp.where(matches, landing[:, :, None], 0), axis=1).reshape(ROWS_DEV)
    recv_perm = (slot_position[:, None] == row_range[None, :]).astype(jnp.bfloat16)
    moved = jnp.dot(
        arrived.reshape(channels, ROWS_DEV), recv_perm, preferred_element_type=jnp.float32
    ).astype(jnp.bfloat16)
    return dual_apply(moved.reshape(2, part_angles, ROWS_DEV), dual_blocks)


def solution(mesh):
    in_specs = (
        P(None, None, ("parts", "blk", "rhs")),
        P(None, "parts"),
        P(None, "parts"),
        P("parts"),
        P(("parts", "blk", "sub"), "rhs"),
        P(("parts", "blk", "sub"), "rhs", None, None),
        P("parts"),
        P(("parts", "blk", "sub"), None, None),
    )
    out_specs = P(None, "rhs", ("parts", "blk", "sub"))
    return jax.shard_map(body, mesh=mesh, in_specs=in_specs, out_specs=out_specs, check_vma=False)
```

profile of v0, /device:TPU:0, one launch (start us, length us, event | category | flops | bytes accessed | tf_op | source)
XLA Modules:
  0.0 402.0 jit_solution(7429419531642535682)
XLA Ops:
  7.3 1.7 reshape.126
  10.1 3.6 copy.111
  13.7 4.8 %gather_fusion.2 = f32[1536,3]{1,0:T(8,128)S(1)} fusion(f32[3,8192]{0,1:T(8,128)} %copy.111, s32[2048]{0:T(1024)S(1)} %pad_clamp_fusion.3), kind=kCustom, calls=%fused_computation.2.clone | custom fusion | bytes 43008 | tf_op jit(solution)/shard_map/jit(_take)/gather | solution.py:22
  19.3 4.9 %gather_fusion.3 = f32[1536,3]{1,0:T(8,128)S(1)} fusion(f32[3,8192]{0,1:T(8,128)} %copy.111, s32[2048]{0:T(1024)S(1)} %pad_clamp_fusion.2), kind=kCustom, calls=%fused_computation.3.clone | custom fusion | bytes 43008 | tf_op jit(solution)/shard_map/jit(_take)/gather | solution.py:21
  25.2 1.4 dynamic_slice.46
  26.5 2.2 copy.112
  30.4 2.2 fusion.56
  32.9 3.9 reshape.128
  40.2 1.4 reshape.129
  41.7 1.4 fusion.45
  43.1 12.1 %all-gather.2.cloned.1.call-done = bf16[2,80,6144]{2,1,0:T(8,128)(2,1)} async-done(((bf16[2,80,1536]{2,1,0:T(8,128)(2,1)}), bf16[2,80,6144]{2,1,0:T(8,128)(2,1)}) %all-gather.2.cloned.1.call-update) | async-done | bytes 1966096 | tf_op jit(solution)/shard_map/all_gather | solution.py:142
  55.2 5.2 %reshape.124 = bf16[2,80,4,1536]{3,2,1,0:T(4,128)(2,1)} reshape(bf16[2,80,6144]{2,1,0:T(8,128)(2,1)} %all-gather.2.cloned.1.call-done) | data formatting | bytes 3932160 | tf_op jit(solution)/shard_map/reshape | solution.py:78
  60.4 1.9 copy.110
  62.8 286.2 %while.13 = (s32[]{:T(128)}, f32[160,1536]{1,0:T(8,128)}, bf16[4,2,80,1536]{3,2,1,0:T(8,128)(2,1)S(1)}, s32[4]{0:T(128)}, s32[]{:T(128)}, /*index=5*/f32[12288]{...) while((s32[]{:T(128)}, f32[160,1536]{1,0:T(8,128)}, ...), condition=%wide.region_1.3_spmd.clone, body=%wide.region_0.2_spmd.clone.sunk | while | flops 1592407552 | bytes 23677272 | solution.py:87
  62.8 1.3 dynamic_slice.70
  65.9 4.8 %gather_fusion = f32[1536,3]{1,0:T(8,128)S(1)} fusion(f32[3,8192]{0,1:T(8,128)} %get-tuple-element.464, s32[2048]{0:T(1024)S(1)} %pad_clamp_fusion.6), kind=kCustom, calls=%fused_computation.1.clone.clone.1 | custom fusion | bytes 43008 | tf_op jit(solution)/shard_map/while/body/eval_jaxpr/jit(_take)/gather | solution.py:21
  71.3 5.2 %gather_fusion.1 = f32[1536,3]{1,0:T(8,128)S(1)} fusion(f32[3,8192]{0,1:T(8,128)} %get-tuple-element.464, s32[2048]{0:T(1024)} %pad_clamp_fusion.7), kind=kCustom, calls=%fused_computation.clone.clone.1 | custom fusion | bytes 43008 | tf_op jit(solution)/shard_map/while/body/eval_jaxpr/jit(_take)/gather | solution.py:22
  77.5 1.1 slice_reduce_fusion.16
  78.6 1.1 slice_reduce_fusion.17
  80.7 47.0 %multiply_convert_fusion.3 = (bf16[1536,1536]{1,0:T(8,128)(2,1)}, bf16[1536,1536]{1,0:T(8,128)(2,1)}) fusion(f32[1536]{0:T(1024)S(1)} %get-tuple-element.402, f32[1536]{0:T(1024)S(1)} %get-tuple-element.408, f32[1536]{0:T(1024)S(1)} %get-tuple-element.409, f32[1536]{0:T(1024)S(1)} %get-tuple-element.410, f32[1536]{0:T(1024)S(1)} %get-tuple-element.411, ...), kind=kLoop, calls=%fused_computation.9.clone.1 | loop fusion | flops 58982400 | bytes 9523200 | tf_op jit(solution)/shard_map/while/body/eval_jaxpr/convert_element_type | solution.py:46
  127.8 6.4 %fusion.71 = f32[160,1536]{1,0:T(8,128)} fusion(bf16[1536,1536]{1,0:T(8,128)(2,1)} %get-tuple-element.420, bf16[1536,1536]{1,0:T(8,128)(2,1)} %get-tuple-element.421, bf16[80,1536]{1,0:T(8,128)(2,1)S(1)} %dynamic-slice_bitcast_fusion.4, bf16[80,1536]{1,0:T(8,128)(2,1)S(1)} %get-tuple-element.422, bf16[80,1536]{1,0:T(8,128)(2,1)S(1)} %get-tuple-element.423, ...), kind=kOutput, calls=%fused_computation.12.clone.1 | convolution fusion | flops 1533247488 | bytes 12140545 | tf_op jit(solution)/shard_map/while/body/eval_jaxpr/dot_general | solution.py:70
  134.2 1.3 dynamic_slice.70
  137.3 4.8 %gather_fusion = f32[1536,3]{1,0:T(8,128)S(1)} fusion(f32[3,8192]{0,1:T(8,128)} %get-tuple-element.464, s32[2048]{0:T(1024)S(1)} %pad_clamp_fusion.6), kind=kCustom, calls=%fused_computation.1.clone.clone.1 | custom fusion | bytes 43008 | tf_op jit(solution)/shard_map/while/body/eval_jaxpr/jit(_take)/gather | solution.py:21
  142.7 5.2 %gather_fusion.1 = f32[1536,3]{1,0:T(8,128)S(1)} fusion(f32[3,8192]{0,1:T(8,128)} %get-tuple-element.464, s32[2048]{0:T(1024)} %pad_clamp_fusion.7), kind=kCustom, calls=%fused_computation.clone.clone.1 | custom fusion | bytes 43008 | tf_op jit(solution)/shard_map/while/body/eval_jaxpr/jit(_take)/gather | solution.py:22
  148.9 1.1 slice_reduce_fusion.16
  150.1 1.1 slice_reduce_fusion.17
  152.1 47.0 %multiply_convert_fusion.3 = (bf16[1536,1536]{1,0:T(8,128)(2,1)}, bf16[1536,1536]{1,0:T(8,128)(2,1)}) fusion(f32[1536]{0:T(1024)S(1)} %get-tuple-element.402, f32[1536]{0:T(1024)S(1)} %get-tuple-element.408, f32[1536]{0:T(1024)S(1)} %get-tuple-element.409, f32[1536]{0:T(1024)S(1)} %get-tuple-element.410, f32[1536]{0:T(1024)S(1)} %get-tuple-element.411, ...), kind=kLoop, calls=%fused_computation.9.clone.1 | loop fusion | flops 58982400 | bytes 9523200 | tf_op jit(solution)/shard_map/while/body/eval_jaxpr/convert_element_type | solution.py:46
  199.2 6.6 %fusion.71 = f32[160,1536]{1,0:T(8,128)} fusion(bf16[1536,1536]{1,0:T(8,128)(2,1)} %get-tuple-element.420, bf16[1536,1536]{1,0:T(8,128)(2,1)} %get-tuple-element.421, bf16[80,1536]{1,0:T(8,128)(2,1)S(1)} %dynamic-slice_bitcast_fusion.4, bf16[80,1536]{1,0:T(8,128)(2,1)S(1)} %get-tuple-element.422, bf16[80,1536]{1,0:T(8,128)(2,1)S(1)} %get-tuple-element.423, ...), kind=kOutput, calls=%fused_computation.12.clone.1 | convolution fusion | flops 1533247488 | bytes 12140545 | tf_op jit(solution)/shard_map/while/body/eval_jaxpr/dot_general | solution.py:70
  205.8 1.3 dynamic_slice.70
  208.9 4.8 %gather_fusion = f32[1536,3]{1,0:T(8,128)S(1)} fusion(f32[3,8192]{0,1:T(8,128)} %get-tuple-element.464, s32[2048]{0:T(1024)S(1)} %pad_clamp_fusion.6), kind=kCustom, calls=%fused_computation.1.clone.clone.1 | custom fusion | bytes 43008 | tf_op jit(solution)/shard_map/while/body/eval_jaxpr/jit(_take)/gather | solution.py:21
  214.3 5.2 %gather_fusion.1 = f32[1536,3]{1,0:T(8,128)S(1)} fusion(f32[3,8192]{0,1:T(8,128)} %get-tuple-element.464, s32[2048]{0:T(1024)} %pad_clamp_fusion.7), kind=kCustom, calls=%fused_computation.clone.clone.1 | custom fusion | bytes 43008 | tf_op jit(solution)/shard_map/while/body/eval_jaxpr/jit(_take)/gather | solution.py:22
  220.5 1.1 slice_reduce_fusion.16
  223.7 47.0 %multiply_convert_fusion.3 = (bf16[1536,1536]{1,0:T(8,128)(2,1)}, bf16[1536,1536]{1,0:T(8,128)(2,1)}) fusion(f32[1536]{0:T(1024)S(1)} %get-tuple-element.402, f32[1536]{0:T(1024)S(1)} %get-tuple-element.408, f32[1536]{0:T(1024)S(1)} %get-tuple-element.409, f32[1536]{0:T(1024)S(1)} %get-tuple-element.410, f32[1536]{0:T(1024)S(1)} %get-tuple-element.411, ...), kind=kLoop, calls=%fused_computation.9.clone.1 | loop fusion | flops 58982400 | bytes 9523200 | tf_op jit(solution)/shard_map/while/body/eval_jaxpr/convert_element_type | solution.py:46
  270.8 6.6 %fusion.71 = f32[160,1536]{1,0:T(8,128)} fusion(bf16[1536,1536]{1,0:T(8,128)(2,1)} %get-tuple-element.420, bf16[1536,1536]{1,0:T(8,128)(2,1)} %get-tuple-element.421, bf16[80,1536]{1,0:T(8,128)(2,1)S(1)} %dynamic-slice_bitcast_fusion.4, bf16[80,1536]{1,0:T(8,128)(2,1)S(1)} %get-tuple-element.422, bf16[80,1536]{1,0:T(8,128)(2,1)S(1)} %get-tuple-element.423, ...), kind=kOutput, calls=%fused_computation.12.clone.1 | convolution fusion | flops 1533247488 | bytes 12140545 | tf_op jit(solution)/shard_map/while/body/eval_jaxpr/dot_general | solution.py:70
  277.4 1.3 dynamic_slice.70
  280.5 4.8 %gather_fusion = f32[1536,3]{1,0:T(8,128)S(1)} fusion(f32[3,8192]{0,1:T(8,128)} %get-tuple-element.464, s32[2048]{0:T(1024)S(1)} %pad_clamp_fusion.6), kind=kCustom, calls=%fused_computation.1.clone.clone.1 | custom fusion | bytes 43008 | tf_op jit(solution)/shard_map/while/body/eval_jaxpr/jit(_take)/gather | solution.py:21
  285.9 5.2 %gather_fusion.1 = f32[1536,3]{1,0:T(8,128)S(1)} fusion(f32[3,8192]{0,1:T(8,128)} %get-tuple-element.464, s32[2048]{0:T(1024)} %pad_clamp_fusion.7), kind=kCustom, calls=%fused_computation.clone.clone.1 | custom fusion | bytes 43008 | tf_op jit(solution)/shard_map/while/body/eval_jaxpr/jit(_take)/gather | solution.py:22
  292.2 1.1 slice_reduce_fusion.16
  293.3 1.1 slice_reduce_fusion.17
  295.3 47.0 %multiply_convert_fusion.3 = (bf16[1536,1536]{1,0:T(8,128)(2,1)}, bf16[1536,1536]{1,0:T(8,128)(2,1)}) fusion(f32[1536]{0:T(1024)S(1)} %get-tuple-element.402, f32[1536]{0:T(1024)S(1)} %get-tuple-element.408, f32[1536]{0:T(1024)S(1)} %get-tuple-element.409, f32[1536]{0:T(1024)S(1)} %get-tuple-element.410, f32[1536]{0:T(1024)S(1)} %get-tuple-element.411, ...), kind=kLoop, calls=%fused_computation.9.clone.1 | loop fusion | flops 58982400 | bytes 9523200 | tf_op jit(solution)/shard_map/while/body/eval_jaxpr/convert_element_type | solution.py:46
  342.4 6.6 %fusion.71 = f32[160,1536]{1,0:T(8,128)} fusion(bf16[1536,1536]{1,0:T(8,128)(2,1)} %get-tuple-element.420, bf16[1536,1536]{1,0:T(8,128)(2,1)} %get-tuple-element.421, bf16[80,1536]{1,0:T(8,128)(2,1)S(1)} %dynamic-slice_bitcast_fusion.4, bf16[80,1536]{1,0:T(8,128)(2,1)S(1)} %get-tuple-element.422, bf16[80,1536]{1,0:T(8,128)(2,1)S(1)} %get-tuple-element.423, ...), kind=kOutput, calls=%fused_computation.12.clone.1 | convolution fusion | flops 1533247488 | bytes 12140545 | tf_op jit(solution)/shard_map/while/body/eval_jaxpr/dot_general | solution.py:70
  349.0 2.6 add.119
  356.0 14.2 %reduce-scatter.2.cloned.1.call-done = f32[2,40,1536]{2,1,0:T(8,128)} async-done(((f32[2,80,1536]{2,1,0:T(8,128)}), f32[2,40,1536]{2,1,0:T(8,128)}) %reduce-scatter.2.cloned.1.call-update) | async-done | bytes 491536 | tf_op jit(solution)/shard_map/reduce_scatter | solution.py:144
  371.2 2.1 fusion.28
  374.4 4.6 %all-to-all-start = ((bf16[80,8,192]{2,0,1:T(8,128)(2,1)}), bf16[80,8,192]{2,0,1:T(8,128)(2,1)S(1)}, u32[]{:S(2)}, u32[]{:S(2)}) async-start(bf16[80,8,192]{2,0,1:T(8,128)(2,1)} %copy.118), calls=%async_computation.1 | async-start | bytes 655360 | tf_op jit(solution)/shard_map/all_to_all | solution.py:165
  379.8 2.1 select_reduce_fusion
  382.4 7.7 %all-to-all-done = bf16[80,8,192]{2,0,1:T(8,128)(2,1)S(1)} async-done(((bf16[80,8,192]{2,0,1:T(8,128)(2,1)}), bf16[80,8,192]{2,0,1:T(8,128)(2,1)S(1)}, u32[]{:S(2)}, u32[]{:S(2)}) %all-to-all-start) | async-done | bytes 245792 | tf_op jit(solution)/shard_map/all_to_all | solution.py:165
  390.5 2.1 fusion.27
  (134 shorter events, 35.8 us)
Async XLA Ops:
  6.5 48.7 %all-gather.2.cloned.1.call-start = ((), (), s32[]{:S(2)}) async-start(), calls=%async_computation.2 | async-start | bytes 2457600 | tf_op jit(solution)/shard_map/all_gather | solution.py:142
  7.3 362.9 %reduce-scatter.2.cloned.1.call-start = ((), (), s32[]{:S(2)}) async-start(), calls=%async_computation.3 | async-start | bytes 1474560 | tf_op jit(solution)/shard_map/reduce_scatter | solution.py:144
  7.3 21.5 %copy-start.5 = (s32[24,2]{0,1:T(2,128)S(1)}, s32[24,2]{0,1:T(2,128)}, u32[]{:S(2)}) copy-start(s32[24,2]{0,1:T(2,128)} %param.16) | copy-start | bytes 580
  36.8 1.4 copy-start
  76.5 4.1 %copy-start.1 = (f32[3,1536]{1,0:T(4,128)S(1)}, f32[3,1536]{1,0:T(4,128)}, u32[]{:S(2)}) copy-start(f32[3,1536]{1,0:T(4,128)} %get-tuple-element.466) | copy-start | bytes 55300 | tf_op jit(solution)/shard_map/while
  76.5 4.1 %copy-start.2 = (f32[3,1536]{1,0:T(4,128)S(1)}, f32[3,1536]{1,0:T(4,128)}, u32[]{:S(2)}) copy-start(f32[3,1536]{1,0:T(4,128)} %get-tuple-element.465) | copy-start | bytes 55300 | tf_op jit(solution)/shard_map/while
  76.5 4.2 %copy-start.4 = (f32[1536]{0:T(1024)S(1)}, f32[1536]{0:T(1024)}, u32[]{:S(2)}) copy-start(f32[1536]{0:T(1024)} %get-tuple-element.462) | copy-start | bytes 18436 | tf_op jit(solution)/shard_map/while
  147.9 4.1 %copy-start.1 = (f32[3,1536]{1,0:T(4,128)S(1)}, f32[3,1536]{1,0:T(4,128)}, u32[]{:S(2)}) copy-start(f32[3,1536]{1,0:T(4,128)} %get-tuple-element.466) | copy-start | bytes 55300 | tf_op jit(solution)/shard_map/while
  147.9 4.1 %copy-start.2 = (f32[3,1536]{1,0:T(4,128)S(1)}, f32[3,1536]{1,0:T(4,128)}, u32[]{:S(2)}) copy-start(f32[3,1536]{1,0:T(4,128)} %get-tuple-element.465) | copy-start | bytes 55300 | tf_op jit(solution)/shard_map/while
  147.9 4.2 %copy-start.4 = (f32[1536]{0:T(1024)S(1)}, f32[1536]{0:T(1024)}, u32[]{:S(2)}) copy-start(f32[1536]{0:T(1024)} %get-tuple-element.462) | copy-start | bytes 18436 | tf_op jit(solution)/shard_map/while
  219.5 4.1 %copy-start.1 = (f32[3,1536]{1,0:T(4,128)S(1)}, f32[3,1536]{1,0:T(4,128)}, u32[]{:S(2)}) copy-start(f32[3,1536]{1,0:T(4,128)} %get-tuple-element.466) | copy-start | bytes 55300 | tf_op jit(solution)/shard_map/while
  219.5 4.1 %copy-start.2 = (f32[3,1536]{1,0:T(4,128)S(1)}, f32[3,1536]{1,0:T(4,128)}, u32[]{:S(2)}) copy-start(f32[3,1536]{1,0:T(4,128)} %get-tuple-element.465) | copy-start | bytes 55300 | tf_op jit(solution)/shard_map/while
  219.5 4.2 %copy-start.4 = (f32[1536]{0:T(1024)S(1)}, f32[1536]{0:T(1024)}, u32[]{:S(2)}) copy-start(f32[1536]{0:T(1024)} %get-tuple-element.462) | copy-start | bytes 18436 | tf_op jit(solution)/shard_map/while
  291.1 4.1 %copy-start.1 = (f32[3,1536]{1,0:T(4,128)S(1)}, f32[3,1536]{1,0:T(4,128)}, u32[]{:S(2)}) copy-start(f32[3,1536]{1,0:T(4,128)} %get-tuple-element.466) | copy-start | bytes 55300 | tf_op jit(solution)/shard_map/while
  291.1 4.1 %copy-start.2 = (f32[3,1536]{1,0:T(4,128)S(1)}, f32[3,1536]{1,0:T(4,128)}, u32[]{:S(2)}) copy-start(f32[3,1536]{1,0:T(4,128)} %get-tuple-element.465) | copy-start | bytes 55300 | tf_op jit(solution)/shard_map/while
  291.1 4.2 %copy-start.4 = (f32[1536]{0:T(1024)S(1)}, f32[1536]{0:T(1024)}, u32[]{:S(2)}) copy-start(f32[1536]{0:T(1024)} %get-tuple-element.462) | copy-start | bytes 18436 | tf_op jit(solution)/shard_map/while
  355.0 27.0 %copy-start.3 = (bf16[24,64,128]{2,1,0:T(8,128)(2,1)S(1)}, bf16[24,64,128]{2,1,0:T(8,128)(2,1)}, u32[]{:S(2)}) copy-start(bf16[24,64,128]{2,1,0:T(8,128)(2,1)} %param.19) | copy-start | bytes 1179652
  374.4 15.8 %all-to-all-start = ((bf16[80,8,192]{2,0,1:T(8,128)(2,1)}), bf16[80,8,192]{2,0,1:T(8,128)(2,1)S(1)}, u32[]{:S(2)}, u32[]{:S(2)}) async-start(bf16[80,8,192]{2,0,1:T(8,128)(2,1)} %copy.118), calls=%async_computation.1 | async-start | bytes 655360 | tf_op jit(solution)/shard_map/all_to_all | solution.py:165
Sparse Core Ops, SparseCore 0:
  8.9 46.2 all-gather.1
  351.7 18.4 reduce-scatter.1
where the time goes:
time: 404 us; the launch traced here: 402 us
  other arithmetic  207 us (51%)
  local copies, waits for them, and re-layouts  105 us (26%)
  waiting for transfers between devices  34.8 us (9%)
  matrix products  34.3 us (8%)
  between operations  13.7 us (3%)
  starting transfers between devices  4.66 us (1%)
    convert_element_type x4, other arithmetic, kernel_tile(): (weight * jnp.cos(phases)).astype(jnp.bfloat16)  188 us
    gather x6, local copies, waits for them, and re-layouts, geometry_span(): minus_tri = jnp.take(tri_cent, minus_ids, axis=1)  26.4 us
    dot_general x4, matrix products, panel_product(): jnp.dot(stacked, tile_pair, preferred_element_type=jnp.float32)  26.2 us
    gather x6, local copies, waits for them, and re-layouts, geometry_span(): plus_tri = jnp.take(tri_cent, plus_ids, axis=1)  24.9 us
    reduce_scatter x1, waiting for transfers between devices, body(): lax.psum_scatter(local_sum, 'rhs', scatter_dimension=1, tiled=True)  14.2 us
    all_gather x1, waiting for transfers between devices, body(): lax.all_gather(currents, 'blk', axis=2, tiled=True)  12.1 us
  transfers between devices with their start and end apart: 3, of which 3 were waited for; matrix products, arithmetic and copies ran while one was open for 11% of the time, Pallas kernels for 0%

commit v1 on v0

v1 whole, which is shorter than its diff:
```python
import functools
import math

import jax
import jax.numpy as jnp
from jax import lax
from jax.experimental import pallas as pl
from jax.experimental.pallas import tpu as pltpu
from jax.sharding import PartitionSpec as P

ROWS_DEV = 1536
BS = 64
LANES = 128
CENTER = 5.0
SOFT2 = 0.1 * 0.1
SPAN2 = 9.0
CHARGE_TERM = 0.5
COS_C = (0.99995979, -19.73104169, 64.67343113, -82.40355036, 45.64655658)
SIN_C = (6.2830558, -41.33121431, 81.36681529, -74.47800454, 32.78140079)
ROUNDER = 12582912.0

F32 = jnp.float32
BF16 = jnp.bfloat16
NT = (((1,), (1,)), ((), ()))
VMEM_LIMIT = 56 * 1024 * 1024


def split3(x):
    h = x.astype(BF16).astype(F32)
    m = (x - h).astype(BF16).astype(F32)
    return h, m, (x - h - m).astype(BF16).astype(F32)


def lookup(table, ids):
    high = table.shape[0] // 3
    width = ids.shape[1]
    low_id = ids & (LANES - 1)
    high_id = ids >> 7
    lows = lax.broadcasted_iota(jnp.int32, (LANES, width), 0) == low_id
    onehot = jnp.where(lows, 1.0, 0.0).astype(BF16)
    picked = jnp.dot(
        table, jnp.concatenate([onehot] * 3, 0), preferred_element_type=F32
    )
    mask = lax.broadcasted_iota(jnp.int32, (high, width), 0) == high_id
    rows = [
        jnp.sum(jnp.where(mask, picked[c * high : (c + 1) * high], 0.0), axis=0, keepdims=True)
        for c in range(3)
    ]
    return jnp.concatenate(rows + [jnp.zeros((5, width), F32)], 0)


def make_table(tri):
    return jnp.concatenate([piece.astype(BF16) for piece in split3(tri)], 1)


def features(table, ids, lens, count_all, is_rows):
    width = ids.shape[1]
    plus, minus = lookup(table, ids[0:1]), lookup(table, ids[1:2])
    row = lax.broadcasted_iota(jnp.int32, (8, width), 0)
    pos = jnp.where(row < 3, 0.5 * (plus + minus) - CENTER, 0.0)
    norm = jnp.sum(pos * pos, axis=0, keepdims=True)
    ends = (minus - plus) * lens + jnp.where(row == 3, lens, 0.0)
    if is_rows:
        scale = 1.0
    else:
        norm = norm + SOFT2
        scale = jnp.where(row == 3, -CHARGE_TERM, 1.0 / SPAN2) / math.sqrt(count_all)
    ends = ends * scale
    h, m, l = split3(pos)
    nh, nm, nl = split3(norm)
    qh, ql, unused = split3(ends)
    norms = jnp.zeros((8, width), F32)
    first = 0 if is_rows else 3
    for k, piece in enumerate((nh, nm, nl)):
        norms = jnp.where(row == first + k, piece, norms)
    ones_at = (row >= 3) & (row < 6) if is_rows else row < 3
    norms = jnp.where(ones_at, 1.0, norms)
    if is_rows:
        h, m, l = -2.0 * h, -2.0 * m, -2.0 * l
        dist_rows = [h, h, m, h, l, m, norms]
        amp_rows = [qh, qh, ql]
    else:
        dist_rows = [h, m, h, l, h, m, norms]
        amp_rows = [qh, ql, qh]
    return dist_rows, amp_rows


def row_features(table, ids, lens, count_all):
    dist_rows, amp_rows = features(table, ids, lens, count_all, True)
    pad = jnp.zeros((48, ids.shape[1]), F32)
    return jnp.transpose(jnp.concatenate(dist_rows + amp_rows + [pad], 0)).astype(BF16)


def col_features(table, ids, lens, count_all):
    dist_rows, amp_rows = features(table, ids, lens, count_all, False)
    width = ids.shape[1]
    zeros = lambda rows: jnp.zeros((rows, width), F32)
    return (
        jnp.concatenate(dist_rows + [zeros(72)], 0).astype(BF16),
        jnp.concatenate([zeros(56)] + amp_rows + [zeros(48)], 0).astype(BF16),
    )


def tile_values(d2, weight):
    inv = lax.rsqrt(d2)
    dist = d2 * inv
    t = dist - ((dist + ROUNDER) - ROUNDER)
    u = t * t
    cosine = COS_C[4]
    for c in COS_C[3::-1]:
        cosine = cosine * u + c
    sine = SIN_C[4]
    for c in SIN_C[3::-1]:
        sine = sine * u + c
    amp = weight * inv
    return (amp * cosine).astype(BF16), ((amp * t) * sine).astype(BF16)


def far_tile(a, bd, bw, x):
    d2 = jnp.dot(a, bd, preferred_element_type=F32)
    weight = jnp.dot(a, bw, preferred_element_type=F32)
    kre, kim = tile_values(d2, weight)
    return lax.dot_general(jnp.concatenate([kre, kim], 0), x, NT, preferred_element_type=F32)


def padded_x(x, rhs, cpad):
    zeros = jnp.zeros((LANES - cpad, x.shape[-1]), BF16)
    rows = []
    for r in range(rhs):
        rows += [x[r], zeros]
    return jnp.concatenate(rows, 0)


def geometry_rows_kernel(count_all, tri_ref, ids_ref, len_ref, a_ref):
    a_ref[...] = row_features(make_table(tri_ref[...]), ids_ref[...], len_ref[...], count_all)


def geometry_cols_kernel(count_all, tri_ref, ids_ref, len_ref, bd_ref, bw_ref):
    bd, bw = col_features(make_table(tri_ref[...]), ids_ref[...], len_ref[...], count_all)
    bd_ref[...] = bd
    bw_ref[...] = bw


def geometry_call(tri, ids, lens, count_all, is_rows, chunk):
    width = ids.shape[1]
    in_specs = [
        pl.BlockSpec(tri.shape, lambda i: (0, 0)),
        pl.BlockSpec((2, chunk), lambda i: (0, i)),
        pl.BlockSpec((1, chunk), lambda i: (0, i)),
    ]
    if is_rows:
        kern = geometry_rows_kernel
        out_specs = pl.BlockSpec((chunk, LANES), lambda i: (i, 0))
        out_shape = jax.ShapeDtypeStruct((width, LANES), BF16)
    else:
        kern = geometry_cols_kernel
        out_specs = [pl.BlockSpec((LANES, chunk), lambda i: (0, i))] * 2
        out_shape = [jax.ShapeDtypeStruct((LANES, width), BF16)] * 2
    return pl.pallas_call(
        functools.partial(kern, count_all),
        grid=(width // chunk,),
        in_specs=in_specs,
        out_specs=out_specs,
        out_shape=out_shape,
        compiler_params=pltpu.CompilerParams(vmem_limit_bytes=VMEM_LIMIT),
    )(tri, ids, lens)


def near_into(acc_re, acc_im, x_full, col_ref, val_ref, block_count):
    row_blocks, per_tile = val_ref.shape[0], val_ref.shape[1]
    lane = lax.broadcasted_iota(jnp.int32, (BS, LANES), 1)

    def one(b, carry):
        total = jnp.zeros((2 * BS, x_full.shape[0]), F32)
        for j in range(per_tile):
            local = lax.rem(col_ref[b, j], block_count)
            pair = lax.div(local, 2)
            odd = lax.rem(local, 2) == 1
            value = val_ref[b, j].astype(F32)
            swapped = jnp.concatenate([value[:, BS:], value[:, :BS]], 1)
            keep = (lane >> 6) == lax.rem(local, 2)
            re_lhs = jnp.where(keep, jnp.where(odd, swapped, value), 0.0)
            im_lhs = jnp.where(keep, jnp.where(odd, value, swapped), 0.0)
            lhs = jnp.concatenate([re_lhs, im_lhs], 0).astype(BF16)
            cols = x_full[:, pl.ds(pl.multiple_of(pair * LANES, LANES), LANES)]
            total = total + lax.dot_general(lhs, cols, NT, preferred_element_type=F32)
        rows = pl.ds(pl.multiple_of(b * BS, BS), BS)
        acc_re[rows, :] = acc_re[rows, :] + total[:BS]
        acc_im[rows, :] = acc_im[rows, :] + total[BS:]
        return carry

    lax.fori_loop(0, row_blocks, one, 0)


def far_kernel(rhs, part_angles, mt, col_ref, a_ref, bd_ref, bw_ref, x_ref, own_ref, val_ref, y_ref, acc_re, acc_im, x_full):
    step = pl.program_id(0)
    cpad = x_ref.shape[2]

    @pl.when(step == 0)
    def _():
        acc_re[...] = jnp.zeros_like(acc_re)
        acc_im[...] = jnp.zeros_like(acc_im)
        x_full[...] = padded_x(own_ref[...], rhs, cpad)
        near_into(acc_re, acc_im, x_full, col_ref, val_ref, own_ref.shape[2] // BS)

    x = padded_x(x_ref[0], rhs, cpad)
    bd, bw = bd_ref[...], bw_ref[...]

    def rows_at(i, carry):
        rows = pl.ds(pl.multiple_of(i * mt, mt), mt)
        out = far_tile(a_ref[rows, :], bd, bw, x)
        acc_re[rows, :] = acc_re[rows, :] + out[:mt]
        acc_im[rows, :] = acc_im[rows, :] + out[mt:]
        return carry

    lax.fori_loop(0, ROWS_DEV // mt, rows_at, 0)

    @pl.when(step == pl.num_programs(0) - 1)
    def _():
        for r in range(rhs):
            lanes = slice(r * LANES, (r + 1) * LANES)
            re = jnp.transpose(acc_re[:, lanes])
            im = jnp.transpose(acc_im[:, lanes])
            pa = part_angles
            y_ref[r, 0:pa, :] = re[:pa] - im[pa : 2 * pa]
            y_ref[r, pa : 2 * pa, :] = re[pa : 2 * pa] + im[:pa]


def far_call(near_col, a, bd, bw, x_all, x_own, near_val, rhs, part_angles):
    groups, unused, cpad, tile = x_all.shape
    nt = 512 if tile % 512 == 0 else 128
    per_group = tile // nt
    mt = 256
    full = lambda array: pl.BlockSpec(array.shape, lambda i, col: (0,) * array.ndim)
    grid_spec = pltpu.PrefetchScalarGridSpec(
        num_scalar_prefetch=1,
        grid=(groups * per_group,),
        in_specs=[
            full(a),
            pl.BlockSpec((LANES, nt), lambda i, col: (0, i)),
            pl.BlockSpec((LANES, nt), lambda i, col: (0, i)),
            pl.BlockSpec((1, rhs, cpad, nt), lambda i, col: (i // per_group, 0, 0, i % per_group)),
            full(x_own),
            full(near_val),
        ],
        out_specs=pl.BlockSpec((rhs, 2 * part_angles, ROWS_DEV), lambda i, col: (0, 0, 0)),
        scratch_shapes=[
            pltpu.VMEM((ROWS_DEV, rhs * LANES), F32),
            pltpu.VMEM((ROWS_DEV, rhs * LANES), F32),
            pltpu.VMEM((rhs * LANES, tile), BF16),
        ],
    )
    return pl.pallas_call(
        functools.partial(far_kernel, rhs, part_angles, mt),
        grid_spec=grid_spec,
        out_shape=jax.ShapeDtypeStruct((rhs, 2 * part_angles, ROWS_DEV), F32),
        compiler_params=pltpu.CompilerParams(vmem_limit_bytes=VMEM_LIMIT),
    )(near_col, a, bd, bw, x_all, x_own, near_val)


def complex_pairs(real_part, imag_part, where_at):
    return jnp.stack(
        [jnp.stack([real_part, -imag_part], where_at), jnp.stack([imag_part, real_part], where_at)],
        where_at,
    )


def dual_apply(moved, dual_blocks):
    angle_count = moved.shape[1]
    row_blocks = dual_blocks.shape[0]
    blocked = moved.reshape(2, angle_count, row_blocks, BS)
    paired = complex_pairs(blocked[0], blocked[1], 0)
    operator = dual_blocks.reshape(row_blocks, BS, 2, BS)
    result = jnp.einsum("bmtn,otabn->oabm", operator, paired, preferred_element_type=jnp.float32)
    return result.reshape(2, angle_count, row_blocks * BS)


def body(currents, tri_cent, edge_tris, edge_len, near_col, near_val, refine_map, dual_blocks):
    blk_count = lax.axis_size("blk")
    rhs_count = lax.axis_size("rhs")
    sub_count = lax.axis_size("sub")
    blk_index = lax.axis_index("blk")
    rhs_index = lax.axis_index("rhs")
    sub_index = lax.axis_index("sub")
    angle_count = currents.shape[1]
    tile_cols = currents.shape[2]
    part_angles = angle_count // rhs_count
    group_cols = tile_cols * rhs_count
    count_all = group_cols * blk_count
    my_owner = blk_index * sub_count + sub_index
    first_row = my_owner * ROWS_DEV

    channels = 2 * part_angles
    cpad = -(-channels // 16) * 16
    x_own = jnp.transpose(
        currents.reshape(2, rhs_count, part_angles, tile_cols), (1, 0, 2, 3)
    ).reshape(rhs_count, channels, tile_cols)
    x_own = jnp.pad(x_own, ((0, 0), (0, cpad - channels), (0, 0)))
    x_all = lax.all_gather(x_own, "blk", axis=0, tiled=False)

    tri = tri_cent.reshape(-1, LANES)
    row_ids = lax.dynamic_slice_in_dim(edge_tris, first_row, ROWS_DEV, 1)
    row_len = lax.dynamic_slice_in_dim(edge_len, first_row, ROWS_DEV, 0)
    take_cols = lambda v, lead: lax.dynamic_index_in_dim(
        v.reshape(lead, blk_count, rhs_count, tile_cols), rhs_index, 2, False
    ).reshape(lead, blk_count * tile_cols)
    col_ids = take_cols(edge_tris, 2)
    col_len = take_cols(edge_len, 1)
    a = geometry_call(tri, row_ids, row_len[None], count_all, True, 512)
    bd, bw = geometry_call(tri, col_ids, col_len, count_all, False, 512)
    local_sum = far_call(near_col, a, bd, bw, x_all, x_own, near_val, rhs_count, part_angles)
    product = lax.psum_scatter(local_sum, "rhs", scatter_dimension=0, tiled=False)
    flat_rows = product.astype(jnp.bfloat16)
    owners = blk_count * sub_count
    slot_rows = ROWS_DEV // owners
    row_range = jnp.arange(ROWS_DEV, dtype=jnp.int32)
    owner_range = jnp.arange(owners, dtype=jnp.int32)
    earlier = (row_range[:, None] > row_range[None, :]).astype(jnp.bfloat16)
    own_map = lax.dynamic_slice_in_dim(refine_map, my_owner * ROWS_DEV, ROWS_DEV, 0)
    target_owner = own_map // ROWS_DEV
    owner_onehot = (target_owner[:, None] == owner_range[None, :]).astype(jnp.bfloat16)
    prior_counts = jnp.dot(earlier, owner_onehot, preferred_element_type=jnp.float32)
    send_rank = jnp.sum(prior_counts * owner_onehot.astype(jnp.float32), axis=1).astype(jnp.int32)
    send_slot = target_owner * slot_rows + send_rank
    send_perm = (send_slot[:, None] == row_range[None, :]).astype(jnp.bfloat16)
    outgoing = jnp.dot(flat_rows, send_perm, preferred_element_type=jnp.float32).astype(
        jnp.bfloat16
    )
    arrived = lax.all_to_all(
        outgoing.reshape(channels, owners, slot_rows),
        ("blk", "sub"),
        split_axis=1,
        concat_axis=1,
        tiled=True,
    )
    source_table = refine_map.reshape(owners, ROWS_DEV)
    bound_here = source_table // ROWS_DEV == my_owner
    recv_counts = jnp.dot(
        bound_here.astype(jnp.bfloat16), jnp.transpose(earlier), preferred_element_type=jnp.float32
    )
    recv_rank = recv_counts.astype(jnp.int32)
    landing = source_table % ROWS_DEV
    slot_range = jnp.arange(slot_rows, dtype=jnp.int32)
    matches = bound_here[:, :, None] & (recv_rank[:, :, None] == slot_range[None, None, :])
    slot_position = jnp.sum(jnp.where(matches, landing[:, :, None], 0), axis=1).reshape(ROWS_DEV)
    recv_perm = (slot_position[:, None] == row_range[None, :]).astype(jnp.bfloat16)
    moved = jnp.dot(
        arrived.reshape(channels, ROWS_DEV), recv_perm, preferred_element_type=jnp.float32
    ).astype(jnp.bfloat16)
    return dual_apply(moved.reshape(2, part_angles, ROWS_DEV), dual_blocks)


def solution(mesh):
    in_specs = (
        P(None, None, ("parts", "blk", "rhs")),
        P(None, "parts"),
        P(None, "parts"),
        P("parts"),
        P(("parts", "blk", "sub"), "rhs"),
        P(("parts", "blk", "sub"), "rhs", None, None),
        P("parts"),
        P(("parts", "blk", "sub"), None, None),
    )
    out_specs = P(None, "rhs", ("parts", "blk", "sub"))
    return jax.shard_map(body, mesh=mesh, in_specs=in_specs, out_specs=out_specs, check_vma=False)
```

time: 404 us -> 178 us (0.44)
  other arithmetic: 207 us -> 2.65 us
  local copies, waits for them, and re-layouts: 105 us -> 13.8 us
  Pallas kernels: 0 us -> 83.4 us
  matrix products: 34.3 us -> 7.31 us
  waiting for transfers between devices: 34.8 us -> 51.5 us
    convert_element_type x5 -> x0, other arithmetic: 189 us -> none  [the longest x4 188 us: kernel_tile(): (weight * jnp.cos(phases)).astype(jnp.bfloat16)]
    pallas_call x0 -> x3, Pallas kernels: none -> 83.4 us  [the longest x1 71.4 us: far_call(): pl.pallas_call(functools.partial(far_kernel, rhs, part_angles, mt), grid_...]
    gather x12 -> x0, local copies, waits for them, and re-layouts: 51.3 us -> none  [the longest x6 26.4 us: geometry_span(): minus_tri = jnp.take(tri_cent, minus_ids, axis=1)]
    dot_general x6 -> x0, matrix products: 28 us -> none  [the longest x4 26.2 us: panel_product(): jnp.dot(stacked, tile_pair, preferred_element_type=jnp.float32)]
    slice x18 -> x0, local copies, waits for them, and re-layouts: 16.8 us -> none  [the longest x5 5.28 us: geometry_span(): minus_ids = lax.dynamic_slice_in_dim(edge_tris[1], first_id, width, 0)]
    all_gather x1, waiting for transfers between devices: 12.1 us -> 26.5 us  [body(): x_all = lax.all_gather(x_own, 'blk', axis=0, tiled=False)]
    reshape x6 -> x4, local copies, waits for them, and re-layouts: 15.3 us -> 5.3 us  [the longest x1 1.85 us: body(): currents.reshape(2, rhs_count, part_angles, tile_cols)]
    dynamic_slice x14 -> x4, local copies, waits for them, and re-layouts: 9.76 us -> 2.87 us  [the longest x1 1.31 us: body(): row_ids = lax.dynamic_slice_in_dim(edge_tris, first_row, ROWS_DEV, 1)]
  transfers between devices with their start and end apart: 3 -> 3, of which waited for: 3 -> 3; matrix products, arithmetic and copies ran while one was open for 11% -> 7% of each run, Pallas kernels for 0% -> 7%
where the time goes in v1:
time: 178 us; the launch traced here: 177 us
  Pallas kernels  83.4 us (47%)
  waiting for transfers between devices  51.5 us (29%)
  local copies, waits for them, and re-layouts  13.8 us (8%)
  between operations  13.6 us (8%)
  matrix products  7.31 us (4%)
  starting transfers between devices  4.67 us (3%)
  other arithmetic  2.65 us (1%)
    pallas_call x1, Pallas kernels, far_call(): pl.pallas_call(functools.partial(far_kernel, rhs, part_angles, mt), grid_...  71.4 us
    all_gather x1, waiting for transfers between devices, body(): x_all = lax.all_gather(x_own, 'blk', axis=0, tiled=False)  26.5 us
    reduce_scatter x1, waiting for transfers between devices, body(): lax.psum_scatter(local_sum, 'rhs', scatter_dimension=0, tiled=False)  17.3 us
    pallas_call x2, Pallas kernels, geometry_call(): pl.pallas_call(functools.partial(kern, count_all), grid=(width // chunk,)...  12 us
    all_to_all x1, waiting for transfers between devices, body(): lax.all_to_all(outgoing.reshape(channels, owners, slot_rows), ('blk', 'su...  7.72 us
    all_to_all x1, starting transfers between devices, body(): lax.all_to_all(outgoing.reshape(channels, owners, slot_rows), ('blk', 'su...  4.63 us
  transfers between devices with their start and end apart: 3, of which 3 were waited for; matrix products, arithmetic and copies ran while one was open for 7% of the time, Pallas kernels for 7%

profile of v1, /device:TPU:0, one launch (start us, length us, event | category | flops | bytes accessed | tf_op | source)
XLA Modules:
  0.0 177.0 jit_solution(9094165937542679454)
XLA Ops:
  6.5 0.0 copy-start.2
  6.5 0.0 all-gather.2.cloned.1.call-start
  6.5 1.9 %copy.48 = bf16[2,2,40,1536]{3,2,0,1:T(8,128)(2,1)} copy(bf16[2,2,40,1536]{3,2,1,0:T(8,128)(2,1)} %bitcast.29) | data formatting | bytes 983040 | tf_op jit(solution)/shard_map/reshape | solution.py:296
  8.4 0.0 all-gather.2.cloned.1.call-update
  8.4 0.0 reduce-scatter.2.cloned.1.call-start
  8.5 0.8 reshape.91
  9.3 0.8 dynamic_slice.18
  10.1 0.6 broadcast_in_dim.10.len_ref
  10.7 1.6 reshape.88.tri_ref
  12.3 1.0 reshape.89
  13.3 0.2 dynamic-slice_reduce_fusion
  13.5 0.6 copy.63
  14.1 0.0 copy-done.2
  14.1 0.7 copy.49.col_ref
  14.8 1.3 constant_dynamic-slice_fusion.1.ids_ref
  16.1 3.3 %shard_map.82.a_ref = bf16[1536,128]{1,0:T(8,128)(2,1)} custom-call(f32[192,128]{1,0:T(8,128)} %reshape.88.tri_ref, s32[2,1536]{1,0:T(2,128)} %constant_dynamic-slice_fusion.1.ids_ref, f32[1,1536]{1,0:T(1,128)} %broadcast_in_dim.10.len_ref), custom_call_target="tpu_custom_call" | custom-call | tf_op jit(solution)/shard_map/pallas_call | solution.py:159
  19.4 0.6 constant_dynamic-slice_fusion
  20.0 8.7 %shard_map.83 = (bf16[128,6144]{1,0:T(8,128)(2,1)}, bf16[128,6144]{1,0:T(8,128)(2,1)}) custom-call(f32[192,128]{1,0:T(8,128)} %reshape.88.tri_ref, s32[2,6144]{1,0:T(2,128)} %bitcast.31, f32[1,6144]{1,0:T(1,128)} %bitcast.32), custom_call_target="tpu_custom_call" | custom-call | tf_op jit(solution)/shard_map/pallas_call | solution.py:159
  28.7 26.5 %all-gather.2.cloned.1.call-done.x_ref = bf16[4,2,80,1536]{3,2,1,0:T(8,128)(2,1)} async-done(((bf16[1,2,80,1536]{3,2,1,0:T(8,128)(2,1)}), bf16[4,2,80,1536]{3,2,1,0:T(8,128)(2,1)}) %all-gather.2.cloned.1.call-update) | async-done | bytes 1966096 | tf_op jit(solution)/shard_map/all_gather | solution.py:299
  55.2 71.4 %shard_map.84 = f32[2,80,1536]{2,1,0:T(8,128)} custom-call(s32[24,2]{1,0:T(8,128)} %copy.49.col_ref, bf16[1536,128]{1,0:T(8,128)(2,1)} %shard_map.82.a_ref, bf16[128,6144]{1,0:T(8,128)(2,1)} %get-tuple-element.7.bd_ref, bf16[128,6144]{1,0:T(8,128)(2,1)} %get-tuple-element.8.bw_ref, bf16[4,2,80,1536]{3,2,1,0:T(8,128)(2,1)} %all-gather.2.cloned.1.call-done.x_ref, ...), custom_call_target="tpu_custom_call" | custom-call | tf_op jit(solution)/shard_map/pallas_call | solution.py:253
  126.6 0.0 reduce-scatter.2.cloned.1.call-update
  126.7 0.0 copy-done.1
  126.8 0.1 ne.62
  126.8 0.1 add_select_fusion.2
  126.9 0.9 fusion.11
  127.8 0.1 convert_add_fusion
  128.0 17.3 %reduce-scatter.2.cloned.1.call-done = f32[1,80,1536]{2,1,0:T(8,128)} async-done(((f32[2,80,1536]{2,1,0:T(8,128)}), f32[1,80,1536]{2,1,0:T(8,128)}) %reduce-scatter.2.cloned.1.call-update) | async-done | bytes 491536 | tf_op jit(solution)/shard_map/reduce_scatter | solution.py:312
  145.2 3.1 %fusion.8 = bf16[80,1536]{1,0:T(8,128)(2,1)S(1)} fusion(s32[1536]{0:T(1024)S(1)} %convert_add_fusion, f32[1,80,1536]{2,1,0:T(8,128)} %reduce-scatter.2.cloned.1.call-done), kind=kOutput, calls=%fused_computation.13 | convolution fusion | flops 380092416 | bytes 743424 | tf_op jit(solution)/shard_map/dot_general | solution.py:326
  148.3 0.3 reshape.95
  148.6 0.0 copy-start
  148.6 0.8 copy.50
  149.4 4.6 %all-to-all-start = ((bf16[80,8,192]{2,0,1:T(8,128)(2,1)}), bf16[80,8,192]{2,0,1:T(8,128)(2,1)S(1)}, u32[]{:S(2)}, u32[]{:S(2)}) async-start(bf16[80,8,192]{2,0,1:T(8,128)(2,1)} %copy.50), calls=%async_computation.1 | async-start | bytes 655360 | tf_op jit(solution)/shard_map/all_to_all | solution.py:329
  154.0 0.9 fusion.10
  154.9 2.1 %select_reduce_fusion = s32[8,192]{1,0:T(8,128)S(1)} fusion(s32[8,1536]{1,0:T(8,128)S(1)} %add_select_fusion, s32[8,1536]{1,0:T(8,128)S(1)} %fusion.10, pred[8,1536]{1,0:T(8,128)(4,1)S(1)} %fusion.18), kind=kLoop, calls=%fused_computation.1 | loop fusion | flops 9435648 | bytes 116736 | tf_op jit(solution)/shard_map/reduce_sum | solution.py:345
  157.0 0.1 eq.72
  157.1 0.0 copy-done
  157.1 0.3 reshape.97
  157.4 7.7 %all-to-all-done = bf16[80,8,192]{2,0,1:T(8,128)(2,1)S(1)} async-done(((bf16[80,8,192]{2,0,1:T(8,128)(2,1)}), bf16[80,8,192]{2,0,1:T(8,128)(2,1)S(1)}, u32[]{:S(2)}, u32[]{:S(2)}) %all-to-all-start) | async-done | bytes 245792 | tf_op jit(solution)/shard_map/all_to_all | solution.py:329
  165.2 0.1 copy.51
  165.3 0.3 reshape.96
  165.5 2.1 %fusion.7 = bf16[80,1536]{1,0:T(8,128)(2,1)S(1)} fusion(bf16[80,1536]{1,0:T(8,128)(2,1)S(1)} %reshape.96, s32[1536]{0:T(1024)S(1)} %eq.72), kind=kOutput, calls=%fused_computation.12 | convolution fusion | flops 379969536 | bytes 497664 | tf_op jit(solution)/shard_map/dot_general | solution.py:347
  167.6 0.2 squeeze.7
  167.8 0.1 copy_negate_fusion
  167.9 0.2 slice.11
  168.1 0.2 maximum_bitcast_fusion
  168.3 0.5 convolution_bitcast_fusion
  168.8 0.3 copy.57
  169.1 1.0 reshape.98
  (9 shorter events, 0.2 us)
Async XLA Ops:
  6.5 7.6 %copy-start.2 = (s32[24,2]{0,1:T(2,128)S(1)}, s32[24,2]{0,1:T(2,128)}, u32[]{:S(2)}) copy-start(s32[24,2]{0,1:T(2,128)} %param.12) | copy-start | bytes 580
  6.5 48.7 %all-gather.2.cloned.1.call-start = ((), (), s32[]{:S(2)}) async-start(), calls=%async_computation.2 | async-start | bytes 2457600 | tf_op jit(solution)/shard_map/all_gather | solution.py:299
  8.4 136.8 %reduce-scatter.2.cloned.1.call-start = ((), (), s32[]{:S(2)}) async-start(), calls=%async_computation.3 | async-start | bytes 1474560 | tf_op jit(solution)/shard_map/reduce_scatter | solution.py:312
  55.2 71.4 %copy-start.1 = (s32[12288]{0:T(1024)S(1)}, s32[12288]{0:T(1024)}, u32[]{:S(2)}) copy-start(s32[12288]{0:T(1024)} %param.14) | copy-start | bytes 147460
  148.6 8.5 %copy-start = (bf16[24,64,128]{2,1,0:T(8,128)(2,1)S(1)}, bf16[24,64,128]{2,1,0:T(8,128)(2,1)}, u32[]{:S(2)}) copy-start(bf16[24,64,128]{2,1,0:T(8,128)(2,1)} %param.15) | copy-start | bytes 1179652
  149.4 15.8 %all-to-all-start = ((bf16[80,8,192]{2,0,1:T(8,128)(2,1)}), bf16[80,8,192]{2,0,1:T(8,128)(2,1)S(1)}, u32[]{:S(2)}, u32[]{:S(2)}) async-start(bf16[80,8,192]{2,0,1:T(8,128)(2,1)} %copy.50), calls=%async_computation.1 | async-start | bytes 655360 | tf_op jit(solution)/shard_map/all_to_all | solution.py:329
Sparse Core Ops, SparseCore 0:
  8.9 46.2 all-gather.1
  126.8 18.4 reduce-scatter.1

commit v2 on v1

v2 whole, which is shorter than its diff:
```python
import functools
import math

import jax
import jax.numpy as jnp
from jax import lax
from jax.experimental import pallas as pl
from jax.experimental.pallas import tpu as pltpu
from jax.sharding import PartitionSpec as P

ROWS_DEV = 1536
BS = 64
LANES = 128
CENTER = 5.0
SOFT2 = 0.1 * 0.1
SPAN2 = 9.0
CHARGE_TERM = 0.5
COS_C = (0.99995979, -19.73104169, 64.67343113, -82.40355036, 45.64655658)
SIN_C = (6.2830558, -41.33121431, 81.36681529, -74.47800454, 32.78140079)
ROUNDER = 12582912.0

F32 = jnp.float32
BF16 = jnp.bfloat16
MESH = pl.DeviceIdType.MESH
NT = (((1,), (1,)), ((), ()))
VMEM_LIMIT = 56 * 1024 * 1024


def split3(x):
    h = x.astype(BF16).astype(F32)
    m = (x - h).astype(BF16).astype(F32)
    return h, m, (x - h - m).astype(BF16).astype(F32)


def lookup(table, ids):
    high = table.shape[0] // 3
    width = ids.shape[1]
    low_id = ids & (LANES - 1)
    high_id = ids >> 7
    lows = lax.broadcasted_iota(jnp.int32, (LANES, width), 0) == low_id
    onehot = jnp.where(lows, 1.0, 0.0).astype(BF16)
    picked = jnp.dot(
        table, jnp.concatenate([onehot] * 3, 0), preferred_element_type=F32
    )
    mask = lax.broadcasted_iota(jnp.int32, (high, width), 0) == high_id
    rows = [
        jnp.sum(jnp.where(mask, picked[c * high : (c + 1) * high], 0.0), axis=0, keepdims=True)
        for c in range(3)
    ]
    return jnp.concatenate(rows + [jnp.zeros((5, width), F32)], 0)


def make_table(tri):
    return jnp.concatenate([piece.astype(BF16) for piece in split3(tri)], 1)


def features(table, ids, lens, count_all, is_rows):
    width = ids.shape[1]
    plus, minus = lookup(table, ids[0:1]), lookup(table, ids[1:2])
    row = lax.broadcasted_iota(jnp.int32, (8, width), 0)
    pos = jnp.where(row < 3, 0.5 * (plus + minus) - CENTER, 0.0)
    norm = jnp.sum(pos * pos, axis=0, keepdims=True)
    ends = (minus - plus) * lens + jnp.where(row == 3, lens, 0.0)
    if is_rows:
        scale = 1.0
    else:
        norm = norm + SOFT2
        scale = jnp.where(row == 3, -CHARGE_TERM, 1.0 / SPAN2) / math.sqrt(count_all)
    ends = ends * scale
    h, m, l = split3(pos)
    nh, nm, nl = split3(norm)
    qh, ql, unused = split3(ends)
    norms = jnp.zeros((8, width), F32)
    first = 0 if is_rows else 3
    for k, piece in enumerate((nh, nm, nl)):
        norms = jnp.where(row == first + k, piece, norms)
    ones_at = (row >= 3) & (row < 6) if is_rows else row < 3
    norms = jnp.where(ones_at, 1.0, norms)
    if is_rows:
        h, m, l = -2.0 * h, -2.0 * m, -2.0 * l
        dist_rows = [h, h, m, h, l, m, norms]
        amp_rows = [qh, qh, ql]
    else:
        dist_rows = [h, m, h, l, h, m, norms]
        amp_rows = [qh, ql, qh]
    return dist_rows, amp_rows


def row_features(table, ids, lens, count_all):
    dist_rows, amp_rows = features(table, ids, lens, count_all, True)
    pad = jnp.zeros((48, ids.shape[1]), F32)
    return jnp.transpose(jnp.concatenate(dist_rows + amp_rows + [pad], 0)).astype(BF16)


def col_features(table, ids, lens, count_all):
    dist_rows, amp_rows = features(table, ids, lens, count_all, False)
    width = ids.shape[1]
    zeros = lambda rows: jnp.zeros((rows, width), F32)
    return (
        jnp.concatenate(dist_rows + [zeros(72)], 0).astype(BF16),
        jnp.concatenate([zeros(56)] + amp_rows + [zeros(48)], 0).astype(BF16),
    )


def tile_values(d2, weight):
    inv = lax.rsqrt(d2)
    dist = d2 * inv
    t = dist - ((dist + ROUNDER) - ROUNDER)
    u = t * t
    cosine = COS_C[4]
    for c in COS_C[3::-1]:
        cosine = cosine * u + c
    sine = SIN_C[4]
    for c in SIN_C[3::-1]:
        sine = sine * u + c
    amp = weight * inv
    return (amp * cosine).astype(BF16), ((amp * t) * sine).astype(BF16)


def far_tile(a, bd, bw, x):
    d2 = jnp.dot(a, bd, preferred_element_type=F32)
    weight = jnp.dot(a, bw, preferred_element_type=F32)
    kre, kim = tile_values(d2, weight)
    return lax.dot_general(jnp.concatenate([kre, kim], 0), x, NT, preferred_element_type=F32)


def combine(real_rows, imag_rows, part_angles):
    lane = lax.broadcasted_iota(jnp.int32, real_rows.shape, 1)
    ahead = pltpu.roll(imag_rows, LANES - part_angles, 1)
    behind = pltpu.roll(imag_rows, part_angles, 1)
    turned = jnp.where(lane < part_angles, -ahead, jnp.where(lane < 2 * part_angles, behind, 0.0))
    return real_rows + turned


def send_slots(own_map, owners):
    width = own_map.shape[1]
    slot_rows = width // owners
    target = lax.div(own_map, jnp.int32(ROWS_DEV))
    before = lax.broadcasted_iota(jnp.int32, (LANES, LANES), 0) < lax.broadcasted_iota(
        jnp.int32, (LANES, LANES), 1
    )
    triangle = jnp.where(before, 1.0, 0.0).astype(BF16)
    running = jnp.zeros((owners, 1), F32)
    ranks = []
    for k in range(width // LANES):
        part = target[:, k * LANES : (k + 1) * LANES]
        hits = lax.broadcasted_iota(jnp.int32, (owners, LANES), 0) == part
        onehot = jnp.where(hits, 1.0, 0.0)
        prior = running + jnp.dot(onehot.astype(BF16), triangle, preferred_element_type=F32)
        ranks.append(jnp.sum(onehot * prior, axis=0, keepdims=True))
        running = running + jnp.sum(onehot, axis=1, keepdims=True)
    return target * slot_rows + jnp.concatenate(ranks, 1).astype(jnp.int32)


def near_kernel(part_angles, col_ref, own_ref, val_ref, y_ref, x_pad, re_buf, im_buf):
    rhs_count, cpad, tile = own_ref.shape
    row_blocks, per_row = val_ref.shape[0], val_ref.shape[1]
    lane = lax.broadcasted_iota(jnp.int32, (BS, LANES), 1)
    if cpad < LANES:
        x_pad[:, cpad:, :] = jnp.zeros((rhs_count, LANES - cpad, tile), BF16)
    x_pad[:, 0:cpad, :] = own_ref[...]

    def near_block(i, carry):
        total = jnp.zeros((2 * BS, rhs_count * LANES), F32)
        for j in range(per_row):
            local = lax.rem(col_ref[i, j], tile // BS)
            odd = lax.rem(local, 2)
            pair = lax.div(local, 2)
            value = val_ref[i, j].astype(F32)
            swapped = jnp.concatenate([value[:, BS:], value[:, :BS]], 1)
            keep = (lane >> 6) == odd
            re_lhs = jnp.where(keep, jnp.where(odd == 1, swapped, value), 0.0)
            im_lhs = jnp.where(keep, jnp.where(odd == 1, value, swapped), 0.0)
            lhs = jnp.concatenate([re_lhs, im_lhs], 0).astype(BF16)
            cols = x_pad[:, :, pl.ds(pl.multiple_of(pair * LANES, LANES), LANES)]
            cols = cols.reshape(rhs_count * LANES, LANES)
            total = total + lax.dot_general(lhs, cols, NT, preferred_element_type=F32)
        rows = pl.ds(pl.multiple_of(i * BS, BS), BS)
        re_buf[rows, :] = total[:BS]
        im_buf[rows, :] = total[BS:]
        return carry

    lax.fori_loop(0, row_blocks, near_block, 0, unroll=4)
    for q in range(rhs_count):
        lanes = slice(q * LANES, (q + 1) * LANES)
        y_ref[q] = combine(re_buf[:, lanes], im_buf[:, lanes], part_angles)


def near_call(near_col, x_own, near_val, part_angles):
    rhs_count, unused, tile = x_own.shape
    vmem = pl.BlockSpec(memory_space=pltpu.VMEM)
    return pl.pallas_call(
        functools.partial(near_kernel, part_angles),
        out_shape=jax.ShapeDtypeStruct((rhs_count, ROWS_DEV, LANES), F32),
        in_specs=[pl.BlockSpec(memory_space=pltpu.SMEM), vmem, vmem],
        out_specs=vmem,
        scratch_shapes=[
            pltpu.VMEM((rhs_count, LANES, tile), BF16),
            pltpu.VMEM((ROWS_DEV, rhs_count * LANES), F32),
            pltpu.VMEM((ROWS_DEV, rhs_count * LANES), F32),
        ],
        compiler_params=pltpu.CompilerParams(vmem_limit_bytes=VMEM_LIMIT),
    )(near_col, x_own, near_val)


def whole_kernel(
    sizes, part_angles,
    tri_ref, row_ids_ref, row_len_ref, col_ids_ref, col_len_ref, own_ref, near_ref, map_ref, dual_ref,
    out_ref,
    a_buf, bd_buf, bw_buf, x_all, acc_re, acc_im, y_own, y_send, y_recv, go_buf, come_buf,
    ag_send, ag_recv, fw_send, fw_recv, y_ssem, y_rsem, p_send, p_recv,
):
    blk_count, rhs_count, sub_count = sizes
    b, r, s = (lax.axis_index(name) for name in ("blk", "rhs", "sub"))
    cpad, tile = own_ref.shape[1], own_ref.shape[2]
    owners = blk_count * sub_count
    me = b * sub_count + s
    count_all = blk_count * rhs_count * tile
    half = rhs_count // sub_count
    slot_rows = ROWS_DEV // owners
    mt = 512
    chunks = ROWS_DEV // mt
    nt = 512 if tile % 512 == 0 else LANES
    per_tile = tile // nt

    barrier = pltpu.get_barrier_semaphore()

    def greet_owner(k, carry):
        o = lax.rem(me + k, owners)
        pl.semaphore_signal(
            barrier, inc=1,
            device_id={"blk": lax.div(o, sub_count), "sub": lax.rem(o, sub_count)},
            device_id_type=MESH,
        )
        return carry

    def greet_rhs(k, carry):
        pl.semaphore_signal(
            barrier, inc=1, device_id={"rhs": lax.rem(r + k, rhs_count)}, device_id_type=MESH
        )
        return carry

    lax.fori_loop(1, owners, greet_owner, 0)
    lax.fori_loop(1, rhs_count, greet_rhs, 0)
    pl.semaphore_wait(barrier, owners - 1 + rhs_count - 1)

    mine = pl.ds(s * half, half)
    theirs = pl.ds((1 - s) * half, half)
    real = pl.ds(0, cpad)

    def gather_copy(k):
        return pltpu.make_async_remote_copy(
            src_ref=own_ref.at[mine],
            dst_ref=x_all.at[b, mine, real],
            send_sem=ag_send.at[k], recv_sem=ag_recv.at[k],
            device_id={"blk": lax.rem(b + k, blk_count)}, device_id_type=MESH,
        )

    def gather_arrival(k):
        source = lax.rem(b - k + blk_count, blk_count)
        return pltpu.make_async_remote_copy(
            src_ref=own_ref.at[mine],
            dst_ref=x_all.at[source, mine, real],
            send_sem=ag_send.at[k], recv_sem=ag_recv.at[k],
            device_id={"blk": source}, device_id_type=MESH,
        )

    def pass_on(k, which):
        source = lax.rem(b - k + blk_count, blk_count)
        return pltpu.make_async_remote_copy(
            src_ref=x_all.at[source, which, real],
            dst_ref=x_all.at[source, which, real],
            send_sem=fw_send.at[k], recv_sem=fw_recv.at[k],
            device_id={"sub": 1 - s}, device_id_type=MESH,
        )

    def start_gather(k, carry):
        gather_copy(k).start()
        return carry

    lax.fori_loop(1, blk_count, start_gather, 0)

    if cpad < LANES:
        x_all[:, :, cpad:, :] = jnp.zeros((blk_count, rhs_count, LANES - cpad, tile), BF16)
    x_all[b, :, 0:cpad, :] = own_ref[...]
    acc_re[...] = jnp.zeros_like(acc_re)
    acc_im[...] = jnp.zeros_like(acc_im)

    table = make_table(tri_ref[...])
    gw = nt

    def row_geometry(i, carry):
        at = pl.ds(pl.multiple_of(i * 512, 512), 512)
        a_buf[at, :] = row_features(table, row_ids_ref[:, at], row_len_ref[:, at], count_all)
        return carry

    lax.fori_loop(0, ROWS_DEV // 512, row_geometry, 0)

    def col_geometry(i, carry):
        at = pl.ds(pl.multiple_of(i * gw, gw), gw)
        bd, bw = col_features(table, col_ids_ref[:, at], col_len_ref[:, at], count_all)
        bd_buf[:, at] = bd
        bw_buf[:, at] = bw
        return carry

    lax.fori_loop(0, blk_count * per_tile, col_geometry, 0)

    def far_step(group, n, rows):
        at = pl.ds(pl.multiple_of(n * nt, nt), nt)
        feats = pl.ds(pl.multiple_of(group * tile + n * nt, nt), nt)
        x = x_all[group, :, :, at].reshape(rhs_count * LANES, nt)
        out = far_tile(a_buf[rows, :], bd_buf[:, feats], bw_buf[:, feats], x)
        acc_re[rows, :] = acc_re[rows, :] + out[:mt]
        acc_im[rows, :] = acc_im[rows, :] + out[mt:]

    def own_tile(i, carry):
        rows = pl.ds(pl.multiple_of(lax.rem(i, chunks) * mt, mt), mt)
        far_step(b, lax.div(i, chunks), rows)
        return carry

    lax.fori_loop(0, per_tile * chunks, own_tile, 0)

    def forward(k, carry):
        gather_arrival(k).wait_recv()
        pass_on(k, mine).start()
        return carry

    lax.fori_loop(1, blk_count, forward, 0)

    def forwarded(k, carry):
        gather_copy(k).wait_send()
        pass_on(k, mine).wait_send()
        pass_on(k, theirs).wait_recv()
        return carry

    lax.fori_loop(1, blk_count, forwarded, 0)

    def y_copy(c, k, outbound):
        rows = pl.ds(pl.multiple_of(c * mt, mt), mt)
        other = lax.rem(r + k, rhs_count) if outbound else lax.rem(r - k + rhs_count, rhs_count)
        return pltpu.make_async_remote_copy(
            src_ref=y_send.at[other, rows],
            dst_ref=y_recv.at[r if outbound else other, rows],
            send_sem=y_ssem.at[c, k], recv_sem=y_rsem.at[c, k],
            device_id={"rhs": other}, device_id_type=MESH,
        )

    def row_chunk(c, carry):
        rows = pl.ds(pl.multiple_of(c * mt, mt), mt)

        def column(i, inner):
            group = lax.rem(b + 1 + lax.div(i, per_tile), blk_count)
            far_step(group, lax.rem(i, per_tile), rows)
            return inner

        lax.fori_loop(0, (blk_count - 1) * per_tile, column, 0)
        own = jnp.zeros((mt, LANES), F32)
        for q in range(rhs_count):
            lanes = slice(q * LANES, (q + 1) * LANES)
            y = combine(acc_re[rows, lanes], acc_im[rows, lanes], part_angles) + near_ref[q, rows, :]
            y_send[q, rows, :] = y.astype(BF16)
            own = own + jnp.where(r == q, y, 0.0)
        y_own[rows, :] = own

        def start(k, inner):
            y_copy(c, k, True).start()
            return inner

        lax.fori_loop(1, rhs_count, start, 0)
        return carry

    lax.fori_loop(0, chunks, row_chunk, 0)

    own_map = map_ref[...]
    slots = send_slots(own_map, owners)
    place = lax.rem(own_map, jnp.int32(ROWS_DEV))
    sub_row = lax.broadcasted_iota(jnp.int32, (LANES, ROWS_DEV), 0)
    marks = jnp.where(
        sub_row == 2 * part_angles,
        place >> 6,
        jnp.where(sub_row == 2 * part_angles + 1, place & 63, 0),
    )
    total = y_own[...] + jnp.transpose(marks.astype(F32))

    for c in range(chunks):
        for k in range(1, rhs_count):
            y_copy(c, k, True).wait_send()
            y_copy(c, k, False).wait_recv()
    for k in range(1, rhs_count):
        total = total + y_recv[lax.rem(r - k + rhs_count, rhs_count)].astype(F32)
    flat = total.astype(BF16)

    def owner_copy(k, outbound):
        o = lax.rem(me + k, owners) if outbound else lax.rem(me - k + owners, owners)
        return pltpu.make_async_remote_copy(
            src_ref=go_buf.at[o],
            dst_ref=come_buf.at[me if outbound else o],
            send_sem=p_send.at[k], recv_sem=p_recv.at[k],
            device_id={"blk": lax.div(o, sub_count), "sub": lax.rem(o, sub_count)},
            device_id_type=MESH,
        )

    def outgoing(o):
        at = lax.broadcasted_iota(jnp.int32, (slot_rows, ROWS_DEV), 0) + o * slot_rows
        perm = jnp.where(at == slots, 1.0, 0.0).astype(BF16)
        return jnp.dot(perm, flat, preferred_element_type=F32).astype(BF16)

    def send_owner(k, carry):
        o = lax.rem(me + k, owners)
        go_buf[o] = outgoing(o)
        owner_copy(k, True).start()
        return carry

    lax.fori_loop(1, owners, send_owner, 0)
    come_buf[me] = outgoing(me)

    def owner_done(k, carry):
        owner_copy(k, True).wait_send()
        owner_copy(k, False).wait_recv()
        return carry

    lax.fori_loop(1, owners, owner_done, 0)

    arrived = come_buf[...].reshape(ROWS_DEV, LANES)
    turned = jnp.transpose(arrived.astype(F32))
    spot = turned[2 * part_angles : 2 * part_angles + 1] * 64.0 + turned[2 * part_angles + 1 : 2 * part_angles + 2]
    spot = spot.astype(jnp.int32)
    wide = 256

    def landing(i, carry):
        at = lax.broadcasted_iota(jnp.int32, (wide, ROWS_DEV), 0) + i * wide
        perm = jnp.where(at == spot, 1.0, 0.0).astype(BF16)
        moved = jnp.dot(perm, arrived, preferred_element_type=F32).astype(BF16)
        rows = []
        for q in range(wide // BS):
            value = dual_ref[i * (wide // BS) + q]
            piece = moved[q * BS : (q + 1) * BS]
            re = jnp.dot(value[:, :BS], piece, preferred_element_type=F32)
            im = jnp.dot(value[:, BS:], piece, preferred_element_type=F32)
            rows.append(combine(re, im, part_angles))
        result = jnp.transpose(jnp.concatenate(rows, 0))
        cols = pl.ds(pl.multiple_of(i * wide, wide), wide)
        out_ref[0, :, cols] = result[:part_angles]
        out_ref[1, :, cols] = result[part_angles : 2 * part_angles]
        return carry

    lax.fori_loop(0, ROWS_DEV // wide, landing, 0)


def body(currents, tri_cent, edge_tris, edge_len, near_col, near_val, refine_map, dual_blocks):
    blk_count = lax.axis_size("blk")
    rhs_count = lax.axis_size("rhs")
    sub_count = lax.axis_size("sub")
    rhs_index = lax.axis_index("rhs")
    angle_count, tile = currents.shape[1], currents.shape[2]
    part_angles = angle_count // rhs_count
    owners = blk_count * sub_count
    first_row = (lax.axis_index("blk") * sub_count + lax.axis_index("sub")) * ROWS_DEV

    channels = 2 * part_angles
    cpad = -(-channels // 16) * 16
    x_own = jnp.transpose(
        currents.reshape(2, rhs_count, part_angles, tile), (1, 0, 2, 3)
    ).reshape(rhs_count, channels, tile)
    x_own = jnp.pad(x_own, ((0, 0), (0, cpad - channels), (0, 0)))

    tri = tri_cent.reshape(-1, LANES)
    row_ids = lax.dynamic_slice_in_dim(edge_tris, first_row, ROWS_DEV, 1)
    row_len = lax.dynamic_slice_in_dim(edge_len, first_row, ROWS_DEV, 0)[None]
    own_map = lax.dynamic_slice_in_dim(refine_map, first_row, ROWS_DEV, 0)[None]
    take_cols = lambda v, lead: lax.dynamic_index_in_dim(
        v.reshape(lead, blk_count, rhs_count, tile), rhs_index, 2, False
    ).reshape(lead, blk_count * tile)
    col_ids = take_cols(edge_tris, 2)
    col_len = take_cols(edge_len, 1)
    near_sum = near_call(near_col, x_own, near_val, part_angles)
    wide = rhs_count * LANES
    chunks = ROWS_DEV // 512
    vmem = pl.BlockSpec(memory_space=pltpu.VMEM)
    dma = lambda *shape: pltpu.SemaphoreType.DMA(shape)
    return pl.pallas_call(
        functools.partial(whole_kernel, (blk_count, rhs_count, sub_count), part_angles),
        out_shape=jax.ShapeDtypeStruct((2, part_angles, ROWS_DEV), F32),
        in_specs=[vmem] * 9,
        out_specs=vmem,
        scratch_shapes=[
            pltpu.VMEM((ROWS_DEV, LANES), BF16),
            pltpu.VMEM((LANES, blk_count * tile), BF16),
            pltpu.VMEM((LANES, blk_count * tile), BF16),
            pltpu.VMEM((blk_count, rhs_count, LANES, tile), BF16),
            pltpu.VMEM((ROWS_DEV, wide), F32),
            pltpu.VMEM((ROWS_DEV, wide), F32),
            pltpu.VMEM((ROWS_DEV, LANES), F32),
            pltpu.VMEM((rhs_count, ROWS_DEV, LANES), BF16),
            pltpu.VMEM((rhs_count, ROWS_DEV, LANES), BF16),
            pltpu.VMEM((owners, ROWS_DEV // owners, LANES), BF16),
            pltpu.VMEM((owners, ROWS_DEV // owners, LANES), BF16),
            dma(blk_count), dma(blk_count), dma(blk_count), dma(blk_count),
            dma(chunks, rhs_count), dma(chunks, rhs_count), dma(owners), dma(owners),
        ],
        compiler_params=pltpu.CompilerParams(
            collective_id=0, has_side_effects=True, vmem_limit_bytes=VMEM_LIMIT
        ),
    )(tri, row_ids, row_len, col_ids, col_len, x_own, near_sum, own_map, dual_blocks)


def solution(mesh):
    in_specs = (
        P(None, None, ("parts", "blk", "rhs")),
        P(None, "parts"),
        P(None, "parts"),
        P("parts"),
        P(("parts", "blk", "sub"), "rhs"),
        P(("parts", "blk", "sub"), "rhs", None, None),
        P("parts"),
        P(("parts", "blk", "sub"), None, None),
    )
    out_specs = P(None, "rhs", ("parts", "blk", "sub"))
    return jax.shard_map(body, mesh=mesh, in_specs=in_specs, out_specs=out_specs, check_vma=False)
```

time: 178 us -> 106 us (0.60)
  waiting for transfers between devices: 51.5 us -> 0 us
  between operations: 13.6 us -> 0.02 us
  matrix products: 7.31 us -> 0 us
  Pallas kernels: 83.4 us -> 90.7 us
  starting transfers between devices: 4.67 us -> 0 us
  other arithmetic: 2.65 us -> 0 us
    all_gather x1 -> x0, waiting for transfers between devices: 26.5 us -> none  [body(): x_all = lax.all_gather(x_own, 'blk', axis=0, tiled=False)]
    reduce_scatter x1 -> x0, waiting for transfers between devices: 17.3 us -> none  [body(): lax.psum_scatter(local_sum, 'rhs', scatter_dimension=0, tiled=False)]
    all_to_all x1 -> x0, waiting for transfers between devices: 7.72 us -> none  [body(): lax.all_to_all(outgoing.reshape(channels, owners, slot_rows), ('blk', 'su...]
    pallas_call x3 -> x2, Pallas kernels: 83.4 us -> 90.7 us  [the longest x1 85.2 us: body(): pl.pallas_call(functools.partial(whole_kernel, (blk_count, rhs_count, sub...]
    dot_general x5 -> x0, matrix products: 7.31 us -> none  [the longest x1 3.06 us: body(): jnp.dot(flat_rows, send_perm, preferred_element_type=jnp.float32)]
    all_to_all x1 -> x0, starting transfers between devices: 4.63 us -> none  [body(): lax.all_to_all(outgoing.reshape(channels, owners, slot_rows), ('blk', 'su...]
    reshape x8 -> x3, local copies, waits for them, and re-layouts: 6.4 us -> 3.68 us  [the longest x1 1.84 us: body(): currents.reshape(2, rhs_count, part_angles, tile)]
    unnamed x8 -> x3, local copies, waits for them, and re-layouts: 1.34 us -> 3.84 us
  transfers between devices with their start and end apart: 3 -> 0, of which waited for: 3 -> 0; matrix products, arithmetic and copies ran while one was open for 7% -> 0% of each run, Pallas kernels for 7% -> 0%
where the time goes in v2:
time: 106 us; the launch traced here: 105 us
  Pallas kernels  90.7 us (86%)
  local copies, waits for them, and re-layouts  14 us (13%)
    pallas_call x1, Pallas kernels, body(): pl.pallas_call(functools.partial(whole_kernel, (blk_count, rhs_count, sub...  85.2 us
    pallas_call x1, Pallas kernels, near_call(): pl.pallas_call(functools.partial(near_kernel, part_angles), out_shape=jax...  5.5 us
    unnamed x3, local copies, waits for them, and re-layouts  3.84 us

profile of v2, /device:TPU:0, one launch (start us, length us, event | category | flops | bytes accessed | tf_op | source)
XLA Modules:
  0.0 104.7 jit_solution(4263417625351245481)
XLA Ops:
  0.0 0.8 dynamic_slice.21
  0.8 0.6 broadcast_in_dim.7.map_ref
  1.4 0.8 dynamic_slice.18
  2.2 0.6 broadcast_in_dim.6.row_len_ref
  2.8 1.3 %constant_dynamic-slice_fusion.1.row_ids_ref = s32[2,1536]{1,0:T(2,128)} fusion(s32[2,12288]{1,0:T(2,128)} %param.10, s32[]{:T(128)S(6)} %select_n.11), kind=kLoop, calls=%fused_computation.2 | loop fusion | bytes 24580 | tf_op jit(solution)/shard_map/dynamic_slice | solution.py:468
  4.1 1.4 %copy.14.col_ref = s32[24,2]{1,0:T(8,128)} copy(s32[24,2]{0,1:T(2,128)} %param.12) | data formatting | bytes 384 | tf_op args[4]
  5.4 0.8 reshape.26
  6.2 0.6 constant_dynamic-slice_fusion
  6.9 1.6 %reshape.23.tri_ref = f32[192,128]{1,0:T(8,128)} reshape(f32[3,8192]{1,0:T(4,128)} %param.9) | data formatting | bytes 196608 | tf_op jit(solution)/shard_map/reshape | solution.py:467
  8.5 1.0 reshape.24
  9.5 0.2 dynamic-slice_reduce_fusion
  9.7 0.6 copy.16
  10.3 1.8 %copy.13 = bf16[2,2,40,1536]{3,2,0,1:T(8,128)(2,1)} copy(bf16[2,2,40,1536]{3,2,1,0:T(8,128)(2,1)} %bitcast.9) | data formatting | bytes 983040 | tf_op jit(solution)/shard_map/reshape | solution.py:463
  12.1 5.5 %shard_map.82.near_ref = f32[2,1536,128]{2,1,0:T(8,128)} custom-call(s32[24,2]{1,0:T(8,128)} %copy.14.col_ref, bf16[2,80,1536]{2,1,0:T(8,128)(2,1)} %bitcast.7, bf16[24,2,64,128]{3,2,1,0:T(8,128)(2,1)} %val_ref.1), custom_call_target="tpu_custom_call" | custom-call | tf_op jit(solution)/shard_map/pallas_call | solution.py:192
  17.6 85.2 %shard_map.83 = f32[2,40,1536]{2,1,0:T(8,128)} custom-call(f32[192,128]{1,0:T(8,128)} %reshape.23.tri_ref, s32[2,1536]{1,0:T(2,128)} %constant_dynamic-slice_fusion.1.row_ids_ref, f32[1,1536]{1,0:T(1,128)} %broadcast_in_dim.6.row_len_ref, s32[2,6144]{1,0:T(2,128)} %bitcast.11, f32[1,6144]{1,0:T(1,128)} %bitcast.12, bf16[2,80,1536]{2,1,0:T(8,128)(2,1)} %bitcast.8, ...), custom_call_target="tpu_custom_call" | custom-call | tf_op jit(solution)/shard_map/pallas_call | solution.py:481
  102.9 1.8 %copy.18 = f32[2,40,1536]{2,1,0:T(8,128)} copy(f32[2,40,1536]{2,1,0:T(8,128)} %shard_map.83) | data formatting | bytes 983040

commit v3 on v2

--- a/solution.py
+++ b/solution.py
@@ -152,13 +152,16 @@
     return target * slot_rows + jnp.concatenate(ranks, 1).astype(jnp.int32)
 
 
-def near_kernel(part_angles, col_ref, own_ref, val_ref, y_ref, x_pad, re_buf, im_buf):
-    rhs_count, cpad, tile = own_ref.shape
+def near_kernel(part_angles, col_ref, cur_ref, val_ref, y_ref, x_ref, x_pad, re_buf, im_buf):
+    rhs_count, cpad, tile = x_ref.shape
     row_blocks, per_row = val_ref.shape[0], val_ref.shape[1]
     lane = lax.broadcasted_iota(jnp.int32, (BS, LANES), 1)
-    if cpad < LANES:
-        x_pad[:, cpad:, :] = jnp.zeros((rhs_count, LANES - cpad, tile), BF16)
-    x_pad[:, 0:cpad, :] = own_ref[...]
+    pa = part_angles
+    for q in range(rhs_count):
+        pieces = [cur_ref[t, q * pa : (q + 1) * pa, :].astype(F32) for t in range(2)]
+        pieces.append(jnp.zeros((LANES - 2 * pa, tile), F32))
+        x_pad[q] = jnp.concatenate(pieces, 0).astype(BF16)
+    x_ref[...] = x_pad[:, 0:cpad, :]
 
     def near_block(i, carry):
         total = jnp.zeros((2 * BS, rhs_count * LANES), F32)
@@ -186,29 +189,32 @@
         y_ref[q] = combine(re_buf[:, lanes], im_buf[:, lanes], part_angles)
 
 
-def near_call(near_col, x_own, near_val, part_angles):
-    rhs_count, unused, tile = x_own.shape
+def near_call(near_col, currents, near_val, rhs_count, cpad):
+    unused, angle_count, tile = currents.shape
     vmem = pl.BlockSpec(memory_space=pltpu.VMEM)
     return pl.pallas_call(
-        functools.partial(near_kernel, part_angles),
-        out_shape=jax.ShapeDtypeStruct((rhs_count, ROWS_DEV, LANES), F32),
+        functools.partial(near_kernel, angle_count // rhs_count),
+        out_shape=[
+            jax.ShapeDtypeStruct((rhs_count, ROWS_DEV, LANES), F32),
+            jax.ShapeDtypeStruct((rhs_count, cpad, tile), BF16),
+        ],
         in_specs=[pl.BlockSpec(memory_space=pltpu.SMEM), vmem, vmem],
-        out_specs=vmem,
+        out_specs=[vmem, vmem],
         scratch_shapes=[
             pltpu.VMEM((rhs_count, LANES, tile), BF16),
             pltpu.VMEM((ROWS_DEV, rhs_count * LANES), F32),
             pltpu.VMEM((ROWS_DEV, rhs_count * LANES), F32),
         ],
         compiler_params=pltpu.CompilerParams(vmem_limit_bytes=VMEM_LIMIT),
-    )(near_col, x_own, near_val)
+    )(near_col, currents, near_val)
 
 
 def whole_kernel(
     sizes, part_angles,
-    tri_ref, row_ids_ref, row_len_ref, col_ids_ref, col_len_ref, own_ref, near_ref, map_ref, dual_ref,
+    tri_ref, ids_ref, len_ref, own_ref, near_ref, map_ref, dual_ref,
     out_ref,
     a_buf, bd_buf, bw_buf, x_all, acc_re, acc_im, y_own, y_send, y_recv, go_buf, come_buf,
-    ag_send, ag_recv, fw_send, fw_recv, y_ssem, y_rsem, p_send, p_recv,
+    ag_send, ag_recv, fw_send, fw_recv, y_ssem, y_rsem, p_send, p_recv, tri_buf,
 ):
     blk_count, rhs_count, sub_count = sizes
     b, r, s = (lax.axis_index(name) for name in ("blk", "rhs", "sub"))
@@ -220,8 +226,8 @@
     slot_rows = ROWS_DEV // owners
     mt = 512
     chunks = ROWS_DEV // mt
-    nt = 512 if tile % 512 == 0 else LANES
-    per_tile = tile // nt
+    nt = tile
+    per_tile = 1
 
     barrier = pltpu.get_barrier_semaphore()
 
@@ -286,24 +292,33 @@
     acc_re[...] = jnp.zeros_like(acc_re)
     acc_im[...] = jnp.zeros_like(acc_im)
 
-    table = make_table(tri_ref[...])
-    gw = nt
+    high = tri_ref.shape[1] // LANES
+    for c in range(3):
+        for h in range(high):
+            tri_buf[c * high + h : c * high + h + 1, :] = tri_ref[c : c + 1, h * LANES : (h + 1) * LANES]
+    table = make_table(tri_buf[...])
+    gw = 512 if tile % 512 == 0 else LANES
+    per_geometry = tile // gw
 
     def row_geometry(i, carry):
         at = pl.ds(pl.multiple_of(i * 512, 512), 512)
-        a_buf[at, :] = row_features(table, row_ids_ref[:, at], row_len_ref[:, at], count_all)
+        full = pl.ds(pl.multiple_of(me * ROWS_DEV + i * 512, 512), 512)
+        a_buf[at, :] = row_features(table, ids_ref[:, full], len_ref[:, full], count_all)
         return carry
 
     lax.fori_loop(0, ROWS_DEV // 512, row_geometry, 0)
 
     def col_geometry(i, carry):
         at = pl.ds(pl.multiple_of(i * gw, gw), gw)
-        bd, bw = col_features(table, col_ids_ref[:, at], col_len_ref[:, at], count_all)
+        group = lax.div(i, per_geometry)
+        first = (group * rhs_count + r) * tile + lax.rem(i, per_geometry) * gw
+        full = pl.ds(pl.multiple_of(first, gw), gw)
+        bd, bw = col_features(table, ids_ref[:, full], len_ref[:, full], count_all)
         bd_buf[:, at] = bd
         bw_buf[:, at] = bw
         return carry
 
-    lax.fori_loop(0, blk_count * per_tile, col_geometry, 0)
+    lax.fori_loop(0, blk_count * per_geometry, col_geometry, 0)
 
     def far_step(group, n, rows):
         at = pl.ds(pl.multiple_of(n * nt, nt), nt)
@@ -371,7 +386,7 @@
 
     lax.fori_loop(0, chunks, row_chunk, 0)
 
-    own_map = map_ref[...]
+    own_map = map_ref[:, pl.ds(pl.multiple_of(me * ROWS_DEV, ROWS_DEV), ROWS_DEV)]
     slots = send_slots(own_map, owners)
     place = lax.rem(own_map, jnp.int32(ROWS_DEV))
     sub_row = lax.broadcasted_iota(jnp.int32, (LANES, ROWS_DEV), 0)
@@ -451,29 +466,13 @@
     blk_count = lax.axis_size("blk")
     rhs_count = lax.axis_size("rhs")
     sub_count = lax.axis_size("sub")
-    rhs_index = lax.axis_index("rhs")
     angle_count, tile = currents.shape[1], currents.shape[2]
     part_angles = angle_count // rhs_count
     owners = blk_count * sub_count
-    first_row = (lax.axis_index("blk") * sub_count + lax.axis_index("sub")) * ROWS_DEV
 
     channels = 2 * part_angles
     cpad = -(-channels // 16) * 16
-    x_own = jnp.transpose(
-        currents.reshape(2, rhs_count, part_angles, tile), (1, 0, 2, 3)
-    ).reshape(rhs_count, channels, tile)
-    x_own = jnp.pad(x_own, ((0, 0), (0, cpad - channels), (0, 0)))
-
-    tri = tri_cent.reshape(-1, LANES)
-    row_ids = lax.dynamic_slice_in_dim(edge_tris, first_row, ROWS_DEV, 1)
-    row_len = lax.dynamic_slice_in_dim(edge_len, first_row, ROWS_DEV, 0)[None]
-    own_map = lax.dynamic_slice_in_dim(refine_map, first_row, ROWS_DEV, 0)[None]
-    take_cols = lambda v, lead: lax.dynamic_index_in_dim(
-        v.reshape(lead, blk_count, rhs_count, tile), rhs_index, 2, False
-    ).reshape(lead, blk_count * tile)
-    col_ids = take_cols(edge_tris, 2)
-    col_len = take_cols(edge_len, 1)
-    near_sum = near_call(near_col, x_own, near_val, part_angles)
+    near_sum, x_own = near_call(near_col, currents, near_val, rhs_count, cpad)
     wide = rhs_count * LANES
     chunks = ROWS_DEV // 512
     vmem = pl.BlockSpec(memory_space=pltpu.VMEM)
@@ -481,7 +480,7 @@
     return pl.pallas_call(
         functools.partial(whole_kernel, (blk_count, rhs_count, sub_count), part_angles),
         out_shape=jax.ShapeDtypeStruct((2, part_angles, ROWS_DEV), F32),
-        in_specs=[vmem] * 9,
+        in_specs=[vmem] * 7,
         out_specs=vmem,
         scratch_shapes=[
             pltpu.VMEM((ROWS_DEV, LANES), BF16),
@@ -497,11 +496,12 @@
             pltpu.VMEM((owners, ROWS_DEV // owners, LANES), BF16),
             dma(blk_count), dma(blk_count), dma(blk_count), dma(blk_count),
             dma(chunks, rhs_count), dma(chunks, rhs_count), dma(owners), dma(owners),
+            pltpu.VMEM((3 * (tri_cent.shape[1] // LANES), LANES), F32),
         ],
         compiler_params=pltpu.CompilerParams(
             collective_id=0, has_side_effects=True, vmem_limit_bytes=VMEM_LIMIT
         ),
-    )(tri, row_ids, row_len, col_ids, col_len, x_own, near_sum, own_map, dual_blocks)
+    )(tri_cent, edge_tris, edge_len[None], x_own, near_sum, refine_map[None], dual_blocks)
 
 
 def solution(mesh):

time: 106 us -> 88.7 us (0.84)
  local copies, waits for them, and re-layouts: 14 us -> 3.2 us
  Pallas kernels: 90.7 us -> 84.7 us
    pallas_call x1, Pallas kernels: 85.2 us -> 79.2 us  [body(): pl.pallas_call(functools.partial(whole_kernel, (blk_count, rhs_count, sub...]
    reshape x4 -> x0, local copies, waits for them, and re-layouts: 5.29 us -> none  [the longest x1 1.84 us: body(): currents.reshape(2, rhs_count, part_angles, tile)]
    dynamic_slice x5 -> x0, local copies, waits for them, and re-layouts: 3.64 us -> none  [the longest x1 1.3 us: body(): row_ids = lax.dynamic_slice_in_dim(edge_tris, first_row, ROWS_DEV, 1)]
    broadcast_in_dim x2 -> x0, local copies, waits for them, and re-layouts: 1.2 us -> none  [the longest x1 0.6 us: body(): own_map = lax.dynamic_slice_in_dim(refine_map, first_row, ROWS_DEV, 0)[None]]
    unnamed x3 -> x2, local copies, waits for them, and re-layouts: 3.84 us -> 3.2 us
where the time goes in v3:
time: 88.7 us; the launch traced here: 87.9 us
  Pallas kernels  84.7 us (95%)
  local copies, waits for them, and re-layouts  3.2 us (4%)
    pallas_call x1, Pallas kernels, body(): pl.pallas_call(functools.partial(whole_kernel, (blk_count, rhs_count, sub...  79.2 us
    pallas_call x1, Pallas kernels, near_call(): pl.pallas_call(functools.partial(near_kernel, angle_count // rhs_count),...  5.52 us
    unnamed x2, local copies, waits for them, and re-layouts  3.2 us

profile of v3, /device:TPU:0, one launch (start us, length us, event | category | flops | bytes accessed | tf_op | source)
XLA Modules:
  0.0 87.9 jit_solution(1966274924946204356)
XLA Ops:
  0.0 1.4 %copy.9.col_ref = s32[24,2]{1,0:T(8,128)} copy(s32[24,2]{0,1:T(2,128)} %param.12) | data formatting | bytes 384 | tf_op args[4]
  1.4 5.5 %shard_map.82 = (f32[2,1536,128]{2,1,0:T(8,128)}, bf16[2,80,1536]{2,1,0:T(8,128)(2,1)}) custom-call(s32[24,2]{1,0:T(8,128)} %copy.9.col_ref, bf16[2,80,1536]{2,1,0:T(8,128)(2,1)} %cur_ref.1, bf16[24,2,64,128]{3,2,1,0:T(8,128)(2,1)} %val_ref.1), custom_call_target="tpu_custom_call" | custom-call | tf_op jit(solution)/shard_map/pallas_call | solution.py:195
  6.9 79.2 %shard_map.83 = f32[2,40,1536]{2,1,0:T(8,128)} custom-call(f32[3,8192]{1,0:T(4,128)} %tri_ref.1, s32[2,12288]{1,0:T(2,128)} %ids_ref.1, f32[1,12288]{1,0:T(1,128)} %bitcast.2, bf16[2,80,1536]{2,1,0:T(8,128)(2,1)} %get-tuple-element.7.own_ref, f32[2,1536,128]{2,1,0:T(8,128)} %get-tuple-element.8.near_ref, s32[1,12288]{1,0:T(1,128)} %bitcast.3, ...), custom_call_target="tpu_custom_call" | custom-call | tf_op jit(solution)/shard_map/pallas_call | solution.py:480
  86.1 1.8 %copy.11 = f32[2,40,1536]{2,1,0:T(8,128)} copy(f32[2,40,1536]{2,1,0:T(8,128)} %shard_map.83) | data formatting | bytes 983040

commit v4 on v3

--- a/solution.py
+++ b/solution.py
@@ -16,7 +16,7 @@
 SPAN2 = 9.0
 CHARGE_TERM = 0.5
 COS_C = (0.99995979, -19.73104169, 64.67343113, -82.40355036, 45.64655658)
-SIN_C = (6.2830558, -41.33121431, 81.36681529, -74.47800454, 32.78140079)
+SIN_C = (6.27863546, -41.09373103, 77.93035288, -56.0864031)
 ROUNDER = 12582912.0
 
 F32 = jnp.float32
@@ -110,8 +110,8 @@
     cosine = COS_C[4]
     for c in COS_C[3::-1]:
         cosine = cosine * u + c
-    sine = SIN_C[4]
-    for c in SIN_C[3::-1]:
+    sine = SIN_C[3]
+    for c in SIN_C[2::-1]:
         sine = sine * u + c
     amp = weight * inv
     return (amp * cosine).astype(BF16), ((amp * t) * sine).astype(BF16)
@@ -183,7 +183,7 @@
         im_buf[rows, :] = total[BS:]
         return carry
 
-    lax.fori_loop(0, row_blocks, near_block, 0, unroll=4)
+    lax.fori_loop(0, row_blocks, near_block, 0, unroll=8)
     for q in range(rhs_count):
         lanes = slice(q * LANES, (q + 1) * LANES)
         y_ref[q] = combine(re_buf[:, lanes], im_buf[:, lanes], part_angles)
@@ -306,7 +306,7 @@
         a_buf[at, :] = row_features(table, ids_ref[:, full], len_ref[:, full], count_all)
         return carry
 
-    lax.fori_loop(0, ROWS_DEV // 512, row_geometry, 0)
+    lax.fori_loop(0, ROWS_DEV // 512, row_geometry, 0, unroll=3)
 
     def col_geometry(i, carry):
         at = pl.ds(pl.multiple_of(i * gw, gw), gw)
@@ -318,7 +318,7 @@
         bw_buf[:, at] = bw
         return carry
 
-    lax.fori_loop(0, blk_count * per_geometry, col_geometry, 0)
+    lax.fori_loop(0, blk_count * per_geometry, col_geometry, 0, unroll=2)
 
     def far_step(group, n, rows):
         at = pl.ds(pl.multiple_of(n * nt, nt), nt)
@@ -459,7 +459,7 @@
         out_ref[1, :, cols] = result[part_angles : 2 * part_angles]
         return carry
 
-    lax.fori_loop(0, ROWS_DEV // wide, landing, 0)
+    lax.fori_loop(0, ROWS_DEV // wide, landing, 0, unroll=2)
 
 
 def body(currents, tri_cent, edge_tris, edge_len, near_col, near_val, refine_map, dual_blocks):

time: 88.7 us -> 85.4 us (0.963)
  Pallas kernels: 84.7 us -> 81.4 us
    pallas_call x1, Pallas kernels: 79.2 us -> 76.5 us  [body(): pl.pallas_call(functools.partial(whole_kernel, (blk_count, rhs_count, sub...]
where the time goes in v4:
time: 85.4 us; the launch traced here: 84.6 us
  Pallas kernels  81.4 us (95%)
  local copies, waits for them, and re-layouts  3.2 us (4%)
    pallas_call x1, Pallas kernels, body(): pl.pallas_call(functools.partial(whole_kernel, (blk_count, rhs_count, sub...  76.5 us
    pallas_call x1, Pallas kernels, near_call(): pl.pallas_call(functools.partial(near_kernel, angle_count // rhs_count),...  4.89 us
    unnamed x2, local copies, waits for them, and re-layouts  3.2 us

profile of v4, /device:TPU:0, one launch (start us, length us, event | category | flops | bytes accessed | tf_op | source)
XLA Modules:
  0.0 84.6 jit_solution(9672124571105210038)
XLA Ops:
  0.0 1.4 %copy.9.col_ref = s32[24,2]{1,0:T(8,128)} copy(s32[24,2]{0,1:T(2,128)} %param.12) | data formatting | bytes 384 | tf_op args[4]
  1.4 4.9 %shard_map.82 = (f32[2,1536,128]{2,1,0:T(8,128)}, bf16[2,80,1536]{2,1,0:T(8,128)(2,1)}) custom-call(s32[24,2]{1,0:T(8,128)} %copy.9.col_ref, bf16[2,80,1536]{2,1,0:T(8,128)(2,1)} %cur_ref.1, bf16[24,2,64,128]{3,2,1,0:T(8,128)(2,1)} %val_ref.1), custom_call_target="tpu_custom_call" | custom-call | tf_op jit(solution)/shard_map/pallas_call | solution.py:195
  6.2 76.5 %shard_map.83 = f32[2,40,1536]{2,1,0:T(8,128)} custom-call(f32[3,8192]{1,0:T(4,128)} %tri_ref.1, s32[2,12288]{1,0:T(2,128)} %ids_ref.1, f32[1,12288]{1,0:T(1,128)} %bitcast.2, bf16[2,80,1536]{2,1,0:T(8,128)(2,1)} %get-tuple-element.7.own_ref, f32[2,1536,128]{2,1,0:T(8,128)} %get-tuple-element.8.near_ref, s32[1,12288]{1,0:T(1,128)} %bitcast.3, ...), custom_call_target="tpu_custom_call" | custom-call | tf_op jit(solution)/shard_map/pallas_call | solution.py:480
  82.8 1.8 %copy.11 = f32[2,40,1536]{2,1,0:T(8,128)} copy(f32[2,40,1536]{2,1,0:T(8,128)} %shard_map.83) | data formatting | bytes 983040
